TPU v7x, 512 devices: a whole 4x8x8 slice. The times are simulated.
512 devices in a mesh: seq: 128 (over z, y, core), head: 4 (over x).
Axes of the slice: x: 4, y: 8, z: 8, core: 2. Of those that a mesh axis runs over, the one named last changes fastest.
Arguments:
- queries: bfloat16 [65536, 1024], P('seq', 'head'), may hold values from -128 to 128
- key_tokens: bfloat16 [65536, 1024], P('seq', 'head'), may hold values from -4 to 4
- value_tokens: bfloat16 [65536, 1024], P('seq', 'head'), may hold values from -48 to 48
- norm_gain: float32 [1024], P('head'), may hold values from 0.25 to 1.75
- out_cotangent: bfloat16 [65536, 1024], P('seq', 'head'), may hold values from -6 to 6
Outputs:
- normed_out: bfloat16 [65536, 1024], P('seq', 'head')
- query_grad: bfloat16 [65536, 1024], P('seq', 'head')
- key_grad: bfloat16 [65536, 1024], P('seq', 'head')
- value_grad: bfloat16 [65536, 1024], P('seq', 'head')
All inputs are finite; a program needn't handle non-finite values.
Results may differ from a plain program's by a relative error of at most 0.017.
Values may be sent and summed in bfloat16 or wider, within the bound.
A program may use at most 64 MiB of HBM per device.

v0:
```python
from functools import reduce

import jax
import jax.numpy as jnp
from jax import lax
from jax.sharding import PartitionSpec as P

HEADS = 8
LEAF = 256
LEVELS = 4


norm_eps = 1e-06


def swapped(value, axis, distance):
    mask = 2**distance
    pairs = [(source, source ^ mask) for source in range(lax.axis_size(axis))]
    return lax.ppermute(value, axis, pairs)


def halve_rows(coarse):
    row_count = coarse.shape[0]
    paired = coarse.astype(jnp.float32).reshape((row_count // 2, 2) + coarse.shape[1:])
    return ((paired[:, 0] + paired[:, 1]) * 0.5).astype(jnp.bfloat16)


def swap_pairs(coarse):
    groups = coarse.shape[0]
    return coarse.reshape((groups // 2, 2) + coarse.shape[1:])[:, ::-1].reshape(coarse.shape)


def spread_rows(coarse):
    row_count = coarse.shape[0]
    return jnp.broadcast_to(0.5 * coarse[:, None], (row_count, 2) + coarse.shape[1:]).reshape(
        (row_count * 2,) + coarse.shape[1:]
    )


def upper_half(position, which_bit):
    return position // 2**which_bit % 2 == 1


def joined(own_part, far_part, is_upper):
    return jnp.where(
        is_upper,
        jnp.concatenate([far_part, own_part], axis=0),
        jnp.concatenate([own_part, far_part], axis=0),
    )


def parted(stacked, is_upper):
    half_rows = stacked.shape[0] // 2
    lower_rows = stacked[:half_rows]
    upper_rows = stacked[half_rows:]
    return (
        jnp.where(is_upper, upper_rows, lower_rows),
        jnp.where(is_upper, lower_rows, upper_rows),
    )


def on_device(queries, key_tokens, value_tokens, norm_gain, out_cotangent):
    tok_rows, width_dev = queries.shape
    head_count = lax.axis_size("head")
    heads_dev = HEADS // head_count
    head_dim = width_dev // heads_dev
    full_width = width_dev * head_count
    score_scale = head_dim ** (-0.5)
    position = lax.axis_index("seq")
    local_levels = (tok_rows // LEAF).bit_length() - 1
    seq_bits = lax.axis_size("seq").bit_length() - 1
    far_levels = [
        height
        for height in range(local_levels + 1, LEVELS + 1)
        if height - 1 - local_levels < seq_bits
    ]
    pyramid_depth = far_levels[-1]
    key_levels = [key_tokens]
    value_levels = [value_tokens]
    for height in range(2, pyramid_depth + 1):
        key_levels.append(halve_rows(key_levels[-1]))
        value_levels.append(halve_rows(value_levels[-1]))
    leaves = tok_rows // LEAF
    blocks = [
        (
            leaves,
            key_tokens.reshape(leaves, LEAF, width_dev),
            value_tokens.reshape(leaves, LEAF, width_dev),
        )
    ]
    height = 1
    groups = tok_rows // (LEAF * 2 ** (height - 1))
    blocks.append(
        (
            groups,
            swap_pairs(key_levels[height - 1].reshape(groups, LEAF, width_dev)),
            swap_pairs(value_levels[height - 1].reshape(groups, LEAF, width_dev)),
        )
    )
    twin_blocks = []
    for height in far_levels:
        which_bit = height - 1 - local_levels
        node_keys = key_levels[height - 1]
        node_values = value_levels[height - 1]
        for lower_bit in range(which_bit):
            came_keys, came_values = swapped((node_keys, node_values), "seq", lower_bit)
            is_upper = upper_half(position, lower_bit)
            node_keys = joined(node_keys, came_keys, is_upper)
            node_values = joined(node_values, came_values, is_upper)
        twin_keys, twin_values = swapped((node_keys, node_values), "seq", which_bit)
        twin_blocks.append((twin_keys, twin_values))
    for twin_keys, twin_values in twin_blocks:
        blocks.append((1, twin_keys[None], twin_values[None]))

    def group_view(tokens, groups):
        return tokens.reshape(groups, tok_rows // groups, heads_dev, head_dim)

    def head_rows(stat):
        return stat.transpose(1, 0, 2).reshape(heads_dev, tok_rows)

    def group_rows(stat, groups):
        return stat.reshape(heads_dev, groups, tok_rows // groups).transpose(1, 0, 2)[..., None]

    scores = []
    for groups, key_block, value_block in blocks:
        key_view = key_block.reshape(groups, LEAF, heads_dev, head_dim)
        scores.append(
            jnp.einsum(
                "grhd,glhd->ghrl",
                group_view(queries, groups),
                key_view,
                preferred_element_type=jnp.float32,
            )
            * score_scale
        )
    row_top = reduce(
        jnp.maximum, [head_rows(jnp.max(level_scores, axis=3)) for level_scores in scores]
    )
    row_total = jnp.zeros((heads_dev, tok_rows), jnp.float32)
    for number in range(len(blocks)):
        groups = blocks[number][0]
        row_total = row_total + head_rows(
            jnp.sum(jnp.exp(scores[number] - group_rows(row_top, groups)), axis=3)
        )
    log_total = row_top + jnp.log(row_total)
    weights = []
    attn_acc = jnp.zeros((tok_rows, width_dev), jnp.float32)
    for number in range(len(blocks)):
        groups, key_block, value_block = blocks[number]
        weight = jnp.exp(scores[number] - group_rows(log_total, groups)).astype(jnp.bfloat16)
        weights.append(weight)
        value_view = value_block.reshape(groups, LEAF, heads_dev, head_dim)
        attn_acc = attn_acc + jnp.einsum(
            "ghrl,glhd->grhd", weight, value_view, preferred_element_type=jnp.float32
        ).reshape(tok_rows, width_dev)
    attn_out = attn_acc.astype(jnp.bfloat16)
    out_float = attn_out.astype(jnp.float32)
    square = lax.psum(jnp.sum(out_float * out_float, axis=1), "head")
    inverse = lax.rsqrt(square / full_width + norm_eps)
    normed_out = (norm_gain[None, :] * out_float * inverse[:, None]).astype(jnp.bfloat16)
    scaled_cot = norm_gain[None, :] * out_cotangent.astype(jnp.float32)
    inner = lax.psum(jnp.sum(scaled_cot * out_float, axis=1), "head")
    grad_attn = (
        inverse[:, None] * scaled_cot
        - out_float * (inverse * inverse * inverse * inner / full_width)[:, None]
    )
    grad_bf = grad_attn.astype(jnp.bfloat16)
    delta = jnp.sum(
        (grad_bf.astype(jnp.float32) * out_float).reshape(tok_rows, heads_dev, head_dim), axis=2
    ).T
    grad_query = jnp.zeros((tok_rows, width_dev), jnp.float32)
    key_cots = [
        jnp.zeros((tok_rows // 2 ** (height - 1), width_dev), jnp.float32)
        for height in range(1, pyramid_depth + 1)
    ]
    value_cots = [
        jnp.zeros((tok_rows // 2 ** (height - 1), width_dev), jnp.float32)
        for height in range(1, pyramid_depth + 1)
    ]
    twin_grads = []
    for number in range(len(blocks)):
        groups, key_block, value_block = blocks[number]
        query_view = group_view(queries, groups)
        grad_view = group_view(grad_bf, groups)
        key_view = key_block.reshape(groups, LEAF, heads_dev, head_dim)
        value_view = value_block.reshape(groups, LEAF, heads_dev, head_dim)
        level_probs = jnp.exp(scores[number] - group_rows(log_total, groups))
        dprob = jnp.einsum(
            "grhd,glhd->ghrl", grad_view, value_view, preferred_element_type=jnp.float32
        )
        dscore = (level_probs * (dprob - group_rows(delta, groups))).astype(jnp.bfloat16)
        grad_query = (
            grad_query
            + jnp.einsum(
                "ghrl,glhd->grhd", dscore, key_view, preferred_element_type=jnp.float32
            ).reshape(tok_rows, width_dev)
            * score_scale
        )
        key_part = (
            jnp.einsum(
                "ghrl,grhd->glhd", dscore, query_view, preferred_element_type=jnp.float32
            ).reshape(groups, LEAF, width_dev)
            * score_scale
        )
        value_part = jnp.einsum(
            "ghrl,grhd->glhd", weights[number], grad_view, preferred_element_type=jnp.float32
        ).reshape(groups, LEAF, width_dev)
        if number == 0:
            key_cots[0] = key_part.reshape(tok_rows, width_dev)
            value_cots[0] = value_part.reshape(tok_rows, width_dev)
        elif number <= local_levels:
            key_cots[number - 1] = key_cots[number - 1] + swap_pairs(key_part).reshape(
                -1, width_dev
            )
            value_cots[number - 1] = value_cots[number - 1] + swap_pairs(value_part).reshape(
                -1, width_dev
            )
        else:
            twin_grads.append((key_part[0], value_part[0]))
    for rank, height in enumerate(far_levels):
        which_bit = height - 1 - local_levels
        twin_keys, twin_values = twin_grads[rank]
        back_keys, back_values = (
            swapped(twin_keys.astype(jnp.bfloat16), "seq", which_bit).astype(twin_keys.dtype),
            swapped(twin_values.astype(jnp.bfloat16), "seq", which_bit).astype(twin_values.dtype),
        )
        for lower_bit in reversed(range(which_bit)):
            is_upper = upper_half(position, lower_bit)
            own_keys, far_keys = parted(back_keys, is_upper)
            own_values, far_values = parted(back_values, is_upper)
            came_keys, came_values = (
                swapped(far_keys.astype(jnp.bfloat16), "seq", lower_bit).astype(far_keys.dtype),
                swapped(far_values.astype(jnp.bfloat16), "seq", lower_bit).astype(far_values.dtype),
            )
            back_keys = own_keys + came_keys
            back_values = own_values + came_values
        key_cots[height - 1] = back_keys
        value_cots[height - 1] = back_values
    for height in range(pyramid_depth, 1, -1):
        key_cots[height - 2] = key_cots[height - 2] + spread_rows(key_cots[height - 1])
        value_cots[height - 2] = value_cots[height - 2] + spread_rows(value_cots[height - 1])
    return (
        normed_out,
        grad_query.astype(jnp.bfloat16),
        key_cots[0].astype(jnp.bfloat16),
        value_cots[0].astype(jnp.bfloat16),
    )


def solution(mesh):
    return jax.shard_map(
        on_device,
        mesh=mesh,
        in_specs=(
            P("seq", "head"),
            P("seq", "head"),
            P("seq", "head"),
            P("head"),
            P("seq", "head"),
        ),
        out_specs=(P("seq", "head"), P("seq", "head"), P("seq", "head"), P("seq", "head")),
        check_vma=False,
    )
```

profile of v0, /device:TPU:1, one launch (start us, length us, event | category | flops | bytes accessed | tf_op | source)
XLA Modules:
  0.0 193.4 jit_solution(5601246595722366029)
XLA Ops:
  0.6 1.2 reshape.506
  4.3 8.8 %collective-permute-start.3 = (bf16[64,256]{1,0:T(8,128)(2,1)}, bf16[64,256]{1,0:T(8,128)(2,1)}, u32[]{:S(2)}, u32[]{:S(2)}) collective-permute-start(bf16[64,256]{1,0:T(8,128)(2,1)} %bitcast.253), channel_id=1, source_target_pairs={{0,4},{4,0},{8,12},{12,8},{16,20},{20,16},{24,28},{28,24},{32,36},... | collective-permute-start | bytes 98312 | tf_op jit(solution)/shard_map/ppermute | solution.py:19
  13.1 2.1 %collective-permute-start.1 = (bf16[128,256]{1,0:T(8,128)(2,1)S(1)}, bf16[128,256]{1,0:T(8,128)(2,1)}, u32[]{:S(2)}, u32[]{:S(2)}) collective-permute-start(bf16[128,256]{1,0:T(8,128)(2,1)S(1)} %bitcast.303), channel_id=1, source_target_pairs={{0,4},{4,0},{8,12},{12,8},{16,20},{20,16},{24,28},{28,24},{32,36},... | collective-permute-start | bytes 196616 | tf_op jit(solution)/shard_map/ppermute | solution.py:19
  15.8 2.4 %collective-permute-start = (bf16[256,256]{1,0:T(8,128)(2,1)}, bf16[256,256]{1,0:T(8,128)(2,1)}, u32[]{:S(2)}, u32[]{:S(2)}) collective-permute-start(bf16[256,256]{1,0:T(8,128)(2,1)} %bitcast.249), channel_id=1, source_target_pairs={{0,4},{4,0},{8,12},{12,8},{16,20},{20,16},{24,28},{28,24},{32,36},... | collective-permute-start | bytes 393224 | tf_op jit(solution)/shard_map/ppermute | solution.py:19
  20.9 1.9 collective-permute-start.9
  22.8 2.4 %collective-permute-start.7 = (bf16[128,256]{1,0:T(8,128)(2,1)S(1)}, bf16[128,256]{1,0:T(8,128)(2,1)}, u32[]{:S(2)}, u32[]{:S(2)}) collective-permute-start(bf16[128,256]{1,0:T(8,128)(2,1)S(1)} %bitcast.305), channel_id=1, source_target_pairs={{0,4},{4,0},{8,12},{12,8},{16,20},{20,16},{24,28},{28,24},{32,36},... | collective-permute-start | bytes 196616 | tf_op jit(solution)/shard_map/ppermute | solution.py:19
  29.7 1.9 collective-permute-start.6
  32.5 1.9 collective-permute-start.4
  35.3 3.4 %collective-permute-start.10 = (bf16[128,256]{1,0:T(8,128)(2,1)S(1)}, bf16[128,256]{1,0:T(8,128)(2,1)S(1)}, u32[]{:S(2)}, u32[]{:S(2)}) collective-permute-start(bf16[128,256]{1,0:T(8,128)(2,1)S(1)} %maximum_select_fusion.5), channel_id=1, source_target_pairs={{0,8},{4,12},{8,0},{12,4},{16,24},{20,28},{24,16},{28,20},{32,40},... | collective-permute-start | bytes 196616 | tf_op jit(solution)/shard_map/ppermute | solution.py:19
  39.6 1.9 collective-permute-start.2
  42.5 3.4 %collective-permute-start.8 = (bf16[256,256]{1,0:T(8,128)(2,1)S(1)}, bf16[256,256]{1,0:T(8,128)(2,1)S(1)}, u32[]{:S(2)}, u32[]{:S(2)}) collective-permute-start(bf16[256,256]{1,0:T(8,128)(2,1)S(1)} %maximum_select_fusion.2), channel_id=1, source_target_pairs={{0,8},{4,12},{8,0},{12,4},{16,24},{20,28},{24,16},{28,20},{32,40},... | collective-permute-start | bytes 393224 | tf_op jit(solution)/shard_map/ppermute | solution.py:19
  45.9 1.9 collective-permute-start.5
  48.5 4.3 %collective-permute-start.11 = (bf16[256,256]{1,0:T(8,128)(2,1)}, bf16[256,256]{1,0:T(8,128)(2,1)}, u32[]{:S(2)}, u32[]{:S(2)}) collective-permute-start(bf16[256,256]{1,0:T(8,128)(2,1)} %maximum_select_fusion.3), channel_id=1, source_target_pairs={{0,16},{4,20},{8,24},{12,28},{16,0},{20,4},{24,8},{28,12},{32,48},... | collective-permute-start | bytes 393224 | tf_op jit(solution)/shard_map/ppermute | solution.py:19
  54.6 1.3 fusion.90
  56.8 1.3 fusion.89
  58.1 1.1 collective-permute-done.5
  59.2 1.7 copy.358
  60.9 1.3 fusion.88
  64.6 1.1 fusion.55
  67.6 1.1 fusion.58
  69.6 1.2 copy.366
  70.8 2.0 %copy.369 = f32[512,256]{1,0:T(8,128)} copy(f32[512,256]{0,1:T(8,128)} %bitcast.267) | data formatting | bytes 1048576 | tf_op jit(solution)/shard_map/reshape | solution.py:155
  72.8 2.0 %copy.372 = f32[512,256]{1,0:T(8,128)} copy(f32[512,256]{0,1:T(8,128)} %bitcast.266) | data formatting | bytes 1048576 | tf_op jit(solution)/shard_map/reshape | solution.py:155
  74.9 2.1 %copy.377 = f32[1,512,2,128]{1,3,2,0:T(8,128)} copy(f32[1,512,2,128]{3,1,2,0:T(8,128)} %bitcast.283) | data formatting | bytes 1048576 | tf_op jit(solution)/shard_map/add | solution.py:153
  76.9 1.7 copy.373
  78.6 2.5 %multiply_reduce_fusion = (f32[512]{0:T(512)S(1)}, f32[2,128,512]{2,1,0:T(8,128)}) fusion(f32[2,128,512]{2,1,0:T(8,128)} %fusion.55, f32[1,512,2,128]{1,3,2,0:T(8,128)} %copy.377, f32[2,128,512]{2,1,0:T(8,128)} %fusion.58, bf16[256,2,128]{0,2,1:T(8,128)(2,1)} %bitcast.293, f32[2,512,256]{1,2,0:T(8,128)S(1)} %get-tuple-element.31, f32[2,512]{1,0:T(2,128)S(1)} %log_add_fusion), kind=kOutput, calls=%fused_computation.87 | convolution fusion | flops 68550144 | bytes 3282944 | tf_op jit(solution)/shard_map/ghrl,glhd->grhd/dot_general | solution.py:153
  81.2 2.0 %copy.375 = f32[512,256]{1,0:T(8,128)} copy(f32[512,256]{0,1:T(8,128)} %bitcast.285) | data formatting | bytes 1048576 | tf_op jit(solution)/shard_map/reshape | solution.py:155
  83.9 2.4 %fusion.27 = (f32[512]{0:T(512)S(1)}, bf16[512,256]{1,0:T(8,128)(2,1)}) fusion(bf16[512,256]{1,0:T(8,128)(2,1)} %param.9, f32[256]{0:T(256)S(1)} %copy-done.42, f32[512,256]{1,0:T(8,128)} %copy.375, f32[512,256]{1,0:T(8,128)} %copy.372, f32[512,256]{1,0:T(8,128)} %copy.369, f32[64,8,2,128]{3,2,1,0:T(2,128)} %bitcast.284), kind=kLoop, calls=%fused_computation.64 | loop fusion | flops 1179136 | bytes 2624512 | tf_op jit(solution)/shard_map/reduce_sum | solution.py:162
  86.3 6.7 %all-reduce = (f32[512]{0:T(512)}, f32[512]{0:T(512)}) all-reduce(f32[512]{0:T(512)S(1)} %get-tuple-element.40, f32[512]{0:T(512)S(1)} %get-tuple-element.13), channel_id=1, replica_groups=mesh['seq'=128,'head'=4] {'head'}, use_global_device_ids=true, to_apply=%region_11.12 | all-reduce | flops 1024 | bytes 8192 | tf_op jit(solution)/shard_map/psum | solution.py:158
  95.0 2.2 %convert_multiply_fusion = (f32[512,256]{1,0:T(8,128)}, bf16[512,256]{1,0:T(8,128)(2,1)}, bf16[512,256]{1,0:T(8,128)(2,1)}) fusion(bf16[512,256]{1,0:T(8,128)(2,1)} %get-tuple-element.14, f32[512]{0:T(512)S(1)} %get-tuple-element.28, bf16[512,256]{1,0:T(8,128)(2,1)} %param.9, f32[256]{0:T(256)S(1)} %copy-done.43, f32[512]{0:T(512)S(1)} %get-tuple-element.29), kind=kLoop, calls=%fused_computation.58 | loop fusion | flops 1572864 | bytes 1577984 | tf_op jit(solution)/shard_map/mul | solution.py:169
  97.2 1.8 copy.480
  99.0 1.7 reshape.494
  100.8 2.1 %reshape.495 = f32[512,2,128]{2,1,0:T(2,128)} reshape(f32[512,256]{1,0:T(8,128)} %get-tuple-element.11) | data formatting | bytes 1048576 | tf_op jit(solution)/shard_map/reshape | solution.py:169
  102.8 2.4 %reduce_sum.79 = f32[512,2]{1,0:T(8,128)} reduce(f32[512,2,128]{2,1,0:T(2,128)} %reshape.495, f32[]{:T(128)} %constant.79.clone.1), dimensions={2}, to_apply=%region_14.15 | reduce | flops 130048 | bytes 528388 | tf_op jit(solution)/shard_map/reduce_sum | solution.py:168
  105.2 1.1 copy.392
  106.3 1.4 fusion.11
  112.1 1.0 convolution_multiply_fusion.7
  115.4 1.1 convolution_multiply_fusion.8
  116.6 1.1 copy.420
  117.7 1.1 fusion.60
  118.9 1.2 fusion.8
  120.3 1.1 convolution_bitcast_fusion
  121.5 1.1 fusion.48
  122.6 1.1 fusion.13
  129.8 4.9 %collective-permute-start.18 = (bf16[256,256]{1,0:T(8,128)(2,1)}, bf16[256,256]{1,0:T(8,128)(2,1)}, u32[]{:S(2)}, u32[]{:S(2)}) collective-permute-start(bf16[256,256]{1,0:T(8,128)(2,1)} %copy.428), channel_id=1, source_target_pairs={{0,4},{4,0},{8,12},{12,8},{16,20},{20,16},{24,28},{28,24},{32,36},... | collective-permute-start | bytes 393224 | tf_op jit(solution)/shard_map/ppermute | solution.py:19
  134.7 1.9 collective-permute-start.12
  136.7 1.9 collective-permute-start.13
  138.6 3.4 %collective-permute-start.19 = (bf16[256,256]{1,0:T(8,128)(2,1)}, bf16[256,256]{1,0:T(8,128)(2,1)S(1)}, u32[]{:S(2)}, u32[]{:S(2)}) collective-permute-start(bf16[256,256]{1,0:T(8,128)(2,1)} %copy.431), channel_id=1, source_target_pairs={{0,8},{4,12},{8,0},{12,4},{16,24},{20,28},{24,16},{28,20},{32,40},... | collective-permute-start | bytes 393224 | tf_op jit(solution)/shard_map/ppermute | solution.py:19
  142.0 2.0 %collective-permute-start.15 = (bf16[256,256]{0,1:T(8,128)(2,1)S(1)}, bf16[256,256]{0,1:T(8,128)(2,1)}, u32[]{:S(2)}, u32[]{:S(2)}) collective-permute-start(bf16[256,256]{0,1:T(8,128)(2,1)S(1)} %bitcast.307), channel_id=1, source_target_pairs={{0,16},{4,20},{8,24},{12,28},{16,0},{20,4},{24,8},{28,12},{32,48},... | collective-permute-start | bytes 393224 | tf_op jit(solution)/shard_map/ppermute | solution.py:19
  144.2 1.3 copy.422
  146.7 1.1 fusion.15
  149.1 1.2 copy.410
  150.3 1.5 copy.389
  151.9 1.9 fusion.36
  154.2 4.2 %collective-permute-start.21 = (bf16[256,256]{0,1:T(8,128)(2,1)S(1)}, bf16[256,256]{0,1:T(8,128)(2,1)S(1)}, u32[]{:S(2)}, u32[]{:S(2)}) collective-permute-start(bf16[256,256]{0,1:T(8,128)(2,1)S(1)} %bitcast.309), channel_id=1, source_target_pairs={{0,16},{4,20},{8,24},{12,28},{16,0},{20,4},{24,8},{28,12},{32,48},... | collective-permute-start | bytes 393224 | tf_op jit(solution)/shard_map/ppermute | solution.py:19
  160.0 3.5 %collective-permute-start.14 = (bf16[128,256]{1,0:T(8,128)(2,1)S(1)}, bf16[128,256]{1,0:T(8,128)(2,1)}, u32[]{:S(2)}, u32[]{:S(2)}) collective-permute-start(bf16[128,256]{1,0:T(8,128)(2,1)S(1)} %select_convert_fusion.5), channel_id=1, source_target_pairs={{0,4},{4,0},{8,12},{12,8},{16,20},{20,16},{24,28},{28,24},{32,36},... | collective-permute-start | bytes 196616 | tf_op jit(solution)/shard_map/ppermute | solution.py:19
  164.5 1.9 collective-permute-start.20
  167.4 1.9 collective-permute-start.16
  169.3 3.0 %collective-permute-done.16 = bf16[128,256]{0,1:T(8,128)(2,1)S(1)} collective-permute-done((bf16[128,256]{0,1:T(8,128)(2,1)S(1)}, bf16[128,256]{0,1:T(8,128)(2,1)S(1)}, u32[]{:S(2)}, u32[]{:S(2)}) %collective-permute-start.16) | collective-permute-done | bytes 65568 | tf_op jit(solution)/shard_map/ppermute | solution.py:19
  172.4 2.3 %collective-permute-start.22 = (bf16[128,256]{0,1:T(8,128)(2,1)S(1)}, bf16[128,256]{0,1:T(8,128)(2,1)S(1)}, u32[]{:S(2)}, u32[]{:S(2)}) collective-permute-start(bf16[128,256]{0,1:T(8,128)(2,1)S(1)} %select_convert_fusion.1), channel_id=1, source_target_pairs={{0,8},{4,12},{8,0},{12,4},{16,24},{20,28},{24,16},{28,20},{32,40},... | collective-permute-start | bytes 196616 | tf_op jit(solution)/shard_map/ppermute | solution.py:19
  174.8 2.6 %collective-permute-done.22 = bf16[128,256]{0,1:T(8,128)(2,1)S(1)} collective-permute-done((bf16[128,256]{0,1:T(8,128)(2,1)S(1)}, bf16[128,256]{0,1:T(8,128)(2,1)S(1)}, u32[]{:S(2)}, u32[]{:S(2)}) %collective-permute-start.22) | collective-permute-done | bytes 65568 | tf_op jit(solution)/shard_map/ppermute | solution.py:19
  177.4 4.7 %collective-permute-start.17 = (bf16[64,256]{0,1:T(8,128)(2,1)S(1)}, bf16[64,256]{0,1:T(8,128)(2,1)S(1)}, u32[]{:S(2)}, u32[]{:S(2)}) collective-permute-start(bf16[64,256]{0,1:T(8,128)(2,1)S(1)} %select_convert_fusion.3), channel_id=1, source_target_pairs={{0,4},{4,0},{8,12},{12,8},{16,20},{20,16},{24,28},{28,24},{32,36},... | collective-permute-start | bytes 98312 | tf_op jit(solution)/shard_map/ppermute | solution.py:19
  182.9 2.5 %collective-permute-start.23 = (bf16[64,256]{0,1:T(8,128)(2,1)S(1)}, bf16[64,256]{0,1:T(8,128)(2,1)S(1)}, u32[]{:S(2)}, u32[]{:S(2)}) collective-permute-start(bf16[64,256]{0,1:T(8,128)(2,1)S(1)} %select_convert_fusion), channel_id=1, source_target_pairs={{0,4},{4,0},{8,12},{12,8},{16,20},{20,16},{24,28},{28,24},{32,36},... | collective-permute-start | bytes 98312 | tf_op jit(solution)/shard_map/ppermute | solution.py:19
  191.0 1.4 reshape.501
  (214 shorter events, 51.8 us)
Async XLA Ops:
  4.3 25.4 %collective-permute-start.3 = (bf16[64,256]{1,0:T(8,128)(2,1)}, bf16[64,256]{1,0:T(8,128)(2,1)}, u32[]{:S(2)}, u32[]{:S(2)}) collective-permute-start(bf16[64,256]{1,0:T(8,128)(2,1)} %bitcast.253), channel_id=1, source_target_pairs={{0,4},{4,0},{8,12},{12,8},{16,20},{20,16},{24,28},{28,24},{32,36},... | collective-permute-start | bytes 98312 | tf_op jit(solution)/shard_map/ppermute | solution.py:19
  13.0 5.2 %copy-start.10 = (bf16[512,256]{1,0:T(8,128)(2,1)S(1)}, bf16[512,256]{1,0:T(8,128)(2,1)}, u32[]{:S(2)}) copy-start(bf16[512,256]{1,0:T(8,128)(2,1)} %param.7) | copy-start | bytes 786436
  13.1 22.2 %collective-permute-start.1 = (bf16[128,256]{1,0:T(8,128)(2,1)S(1)}, bf16[128,256]{1,0:T(8,128)(2,1)}, u32[]{:S(2)}, u32[]{:S(2)}) collective-permute-start(bf16[128,256]{1,0:T(8,128)(2,1)S(1)} %bitcast.303), channel_id=1, source_target_pairs={{0,4},{4,0},{8,12},{12,8},{16,20},{20,16},{24,28},{28,24},{32,36},... | collective-permute-start | bytes 196616 | tf_op jit(solution)/shard_map/ppermute | solution.py:19
  15.8 32.7 %collective-permute-start = (bf16[256,256]{1,0:T(8,128)(2,1)}, bf16[256,256]{1,0:T(8,128)(2,1)}, u32[]{:S(2)}, u32[]{:S(2)}) collective-permute-start(bf16[256,256]{1,0:T(8,128)(2,1)} %bitcast.249), channel_id=1, source_target_pairs={{0,4},{4,0},{8,12},{12,8},{16,20},{20,16},{24,28},{28,24},{32,36},... | collective-permute-start | bytes 393224 | tf_op jit(solution)/shard_map/ppermute | solution.py:19
  20.2 5.1 %copy-start.9 = (bf16[512,256]{1,0:T(8,128)(2,1)S(1)}, bf16[512,256]{1,0:T(8,128)(2,1)}, u32[]{:S(2)}) copy-start(bf16[512,256]{1,0:T(8,128)(2,1)} %param.6) | copy-start | bytes 786436
  20.9 11.6 %collective-permute-start.9 = (bf16[64,256]{1,0:T(8,128)(2,1)}, bf16[64,256]{1,0:T(8,128)(2,1)}, u32[]{:S(2)}, u32[]{:S(2)}) collective-permute-start(bf16[64,256]{1,0:T(8,128)(2,1)} %bitcast.252), channel_id=1, source_target_pairs={{0,4},{4,0},{8,12},{12,8},{16,20},{20,16},{24,28},{28,24},{32,36},... | collective-permute-start | bytes 98312 | tf_op jit(solution)/shard_map/ppermute | solution.py:19
  22.8 16.8 %collective-permute-start.7 = (bf16[128,256]{1,0:T(8,128)(2,1)S(1)}, bf16[128,256]{1,0:T(8,128)(2,1)}, u32[]{:S(2)}, u32[]{:S(2)}) collective-permute-start(bf16[128,256]{1,0:T(8,128)(2,1)S(1)} %bitcast.305), channel_id=1, source_target_pairs={{0,4},{4,0},{8,12},{12,8},{16,20},{20,16},{24,28},{28,24},{32,36},... | collective-permute-start | bytes 196616 | tf_op jit(solution)/shard_map/ppermute | solution.py:19
  25.3 2.1 %copy-start.13 = (bf16[2,256,2,128]{3,2,1,0:T(2,128)(2,1)}, bf16[2,256,2,128]{3,2,1,0:T(2,128)(2,1)S(1)}, u32[]{:S(2)}) copy-start(bf16[2,256,2,128]{3,2,1,0:T(2,128)(2,1)S(1)} %reshape_reshape.34) | copy-start | bytes 786436
  25.4 1.0 copy-start.35
  26.6 0.9 copy-start.6
  29.7 24.2 %collective-permute-start.6 = (bf16[256,256]{1,0:T(8,128)(2,1)S(1)}, bf16[256,256]{1,0:T(8,128)(2,1)S(1)}, u32[]{:S(2)}, u32[]{:S(2)}) collective-permute-start(bf16[256,256]{1,0:T(8,128)(2,1)S(1)} %bitcast.308), channel_id=1, source_target_pairs={{0,4},{4,0},{8,12},{12,8},{16,20},{20,16},{24,28},{28,24},{32,36},... | collective-permute-start | bytes 393224 | tf_op jit(solution)/shard_map/ppermute | solution.py:19
  32.5 10.0 %collective-permute-start.4 = (bf16[128,256]{1,0:T(8,128)(2,1)S(1)}, bf16[128,256]{1,0:T(8,128)(2,1)S(1)}, u32[]{:S(2)}, u32[]{:S(2)}) collective-permute-start(bf16[128,256]{1,0:T(8,128)(2,1)S(1)} %maximum_select_fusion.4), channel_id=1, source_target_pairs={{0,8},{4,12},{8,0},{12,4},{16,24},{20,28},{24,16},{28,20},{32,40},... | collective-permute-start | bytes 196616 | tf_op jit(solution)/shard_map/ppermute | solution.py:19
  35.3 10.6 %collective-permute-start.10 = (bf16[128,256]{1,0:T(8,128)(2,1)S(1)}, bf16[128,256]{1,0:T(8,128)(2,1)S(1)}, u32[]{:S(2)}, u32[]{:S(2)}) collective-permute-start(bf16[128,256]{1,0:T(8,128)(2,1)S(1)} %maximum_select_fusion.5), channel_id=1, source_target_pairs={{0,8},{4,12},{8,0},{12,4},{16,24},{20,28},{24,16},{28,20},{32,40},... | collective-permute-start | bytes 196616 | tf_op jit(solution)/shard_map/ppermute | solution.py:19
  39.6 16.3 %collective-permute-start.2 = (bf16[256,256]{1,0:T(8,128)(2,1)S(1)}, bf16[256,256]{1,0:T(8,128)(2,1)S(1)}, u32[]{:S(2)}, u32[]{:S(2)}) collective-permute-start(bf16[256,256]{1,0:T(8,128)(2,1)S(1)} %maximum_select_fusion), channel_id=1, source_target_pairs={{0,8},{4,12},{8,0},{12,4},{16,24},{20,28},{24,16},{28,20},{32,40},... | collective-permute-start | bytes 393224 | tf_op jit(solution)/shard_map/ppermute | solution.py:19
  42.5 13.5 %collective-permute-start.8 = (bf16[256,256]{1,0:T(8,128)(2,1)S(1)}, bf16[256,256]{1,0:T(8,128)(2,1)S(1)}, u32[]{:S(2)}, u32[]{:S(2)}) collective-permute-start(bf16[256,256]{1,0:T(8,128)(2,1)S(1)} %maximum_select_fusion.2), channel_id=1, source_target_pairs={{0,8},{4,12},{8,0},{12,4},{16,24},{20,28},{24,16},{28,20},{32,40},... | collective-permute-start | bytes 393224 | tf_op jit(solution)/shard_map/ppermute | solution.py:19
  45.9 13.3 %collective-permute-start.5 = (bf16[256,256]{1,0:T(8,128)(2,1)S(1)}, bf16[256,256]{1,0:T(8,128)(2,1)}, u32[]{:S(2)}, u32[]{:S(2)}) collective-permute-start(bf16[256,256]{1,0:T(8,128)(2,1)S(1)} %maximum_select_fusion.1), channel_id=1, source_target_pairs={{0,16},{4,20},{8,24},{12,28},{16,0},{20,4},{24,8},{28,12},{32,48},... | collective-permute-start | bytes 393224 | tf_op jit(solution)/shard_map/ppermute | solution.py:19
  48.5 28.4 %collective-permute-start.11 = (bf16[256,256]{1,0:T(8,128)(2,1)}, bf16[256,256]{1,0:T(8,128)(2,1)}, u32[]{:S(2)}, u32[]{:S(2)}) collective-permute-start(bf16[256,256]{1,0:T(8,128)(2,1)} %maximum_select_fusion.3), channel_id=1, source_target_pairs={{0,16},{4,20},{8,24},{12,28},{16,0},{20,4},{24,8},{28,12},{32,48},... | collective-permute-start | bytes 393224 | tf_op jit(solution)/shard_map/ppermute | solution.py:19
  56.0 0.8 copy-start.28
  62.2 1.2 copy-start
  62.2 1.5 copy-start.2
  63.7 0.9 copy-start.33
  64.6 1.1 copy-start.16
  65.8 1.0 copy-start.18
  66.7 0.9 copy-start.31
  106.3 2.4 %copy-start.30 = (bf16[256,256]{0,1:T(8,128)(2,1)S(1)}, bf16[256,256]{0,1:T(8,128)(2,1)}, u32[]{:S(2)}) copy-start(bf16[256,256]{0,1:T(8,128)(2,1)} %copy.358) | copy-start | bytes 393220
  107.7 2.0 %copy-start.3 = (f32[2,512,256]{1,2,0:T(8,128)S(1)}, f32[2,512,256]{1,2,0:T(8,128)}, u32[]{:S(2)}) copy-start(f32[2,512,256]{1,2,0:T(8,128)} %get-tuple-element.33) | copy-start | bytes 3145732
  108.7 1.0 copy-start.4
  109.7 1.0 copy-start.34
  110.7 1.4 copy-start.29
  111.1 2.0 %copy-start.1 = (f32[2,512,256]{1,2,0:T(8,128)S(1)}, f32[2,512,256]{1,2,0:T(8,128)}, u32[]{:S(2)}) copy-start(f32[2,512,256]{1,2,0:T(8,128)} %get-tuple-element.35) | copy-start | bytes 3145732
  113.1 1.0 copy-start.32
  115.4 1.1 copy-start.15
  117.7 1.1 copy-start.19
  118.9 1.2 copy-start.17
  120.3 1.1 copy-start.14
  121.5 1.1 copy-start.7
  122.6 1.1 copy-start.23
  123.7 1.0 copy-start.39
  123.7 1.8 copy-start.24
  125.5 1.0 copy-start.36
  125.5 1.8 copy-start.25
  127.3 1.0 copy-start.37
  127.3 1.8 copy-start.38
  127.3 14.7 %copy-start.40 = (bf16[2,256,128]{1,2,0:T(8,128)(2,1)S(1)}, bf16[2,256,128]{1,2,0:T(8,128)(2,1)}, u32[]{:S(2)}) copy-start(bf16[2,256,128]{1,2,0:T(8,128)(2,1)} %fusion.19) | copy-start | bytes 393220
  128.3 15.7 %copy-start.20 = (f32[2,2,128,256]{3,2,1,0:T(8,128)S(1)}, f32[2,2,128,256]{3,2,1,0:T(8,128)}, u32[]{:S(2)}) copy-start(f32[2,2,128,256]{3,2,1,0:T(8,128)} %fusion.60) | copy-start | bytes 1572868
  129.8 58.7 %collective-permute-start.18 = (bf16[256,256]{1,0:T(8,128)(2,1)}, bf16[256,256]{1,0:T(8,128)(2,1)}, u32[]{:S(2)}, u32[]{:S(2)}) collective-permute-start(bf16[256,256]{1,0:T(8,128)(2,1)} %copy.428), channel_id=1, source_target_pairs={{0,4},{4,0},{8,12},{12,8},{16,20},{20,16},{24,28},{28,24},{32,36},... | collective-permute-start | bytes 393224 | tf_op jit(solution)/shard_map/ppermute | solution.py:19
  134.7 55.3 %collective-permute-start.12 = (bf16[256,256]{1,0:T(8,128)(2,1)}, bf16[256,256]{1,0:T(8,128)(2,1)S(1)}, u32[]{:S(2)}, u32[]{:S(2)}) collective-permute-start(bf16[256,256]{1,0:T(8,128)(2,1)} %copy.413), channel_id=1, source_target_pairs={{0,4},{4,0},{8,12},{12,8},{16,20},{20,16},{24,28},{28,24},{32,36},... | collective-permute-start | bytes 393224 | tf_op jit(solution)/shard_map/ppermute | solution.py:19
  136.7 17.5 %collective-permute-start.13 = (bf16[256,256]{1,0:T(8,128)(2,1)}, bf16[256,256]{1,0:T(8,128)(2,1)}, u32[]{:S(2)}, u32[]{:S(2)}) collective-permute-start(bf16[256,256]{1,0:T(8,128)(2,1)} %copy.416), channel_id=1, source_target_pairs={{0,8},{4,12},{8,0},{12,4},{16,24},{20,28},{24,16},{28,20},{32,40},... | collective-permute-start | bytes 393224 | tf_op jit(solution)/shard_map/ppermute | solution.py:19
  138.6 20.7 %collective-permute-start.19 = (bf16[256,256]{1,0:T(8,128)(2,1)}, bf16[256,256]{1,0:T(8,128)(2,1)S(1)}, u32[]{:S(2)}, u32[]{:S(2)}) collective-permute-start(bf16[256,256]{1,0:T(8,128)(2,1)} %copy.431), channel_id=1, source_target_pairs={{0,8},{4,12},{8,0},{12,4},{16,24},{20,28},{24,16},{28,20},{32,40},... | collective-permute-start | bytes 393224 | tf_op jit(solution)/shard_map/ppermute | solution.py:19
  142.0 22.5 %collective-permute-start.15 = (bf16[256,256]{0,1:T(8,128)(2,1)S(1)}, bf16[256,256]{0,1:T(8,128)(2,1)}, u32[]{:S(2)}, u32[]{:S(2)}) collective-permute-start(bf16[256,256]{0,1:T(8,128)(2,1)S(1)} %bitcast.307), channel_id=1, source_target_pairs={{0,16},{4,20},{8,24},{12,28},{16,0},{20,4},{24,8},{28,12},{32,48},... | collective-permute-start | bytes 393224 | tf_op jit(solution)/shard_map/ppermute | solution.py:19
  144.2 1.3 copy-start.8
  145.6 1.0 copy-start.12
  145.6 1.1 copy-start.21
  146.7 1.1 copy-start.22
  150.3 1.6 copy-start.26
  150.3 1.6 copy-start.27
  151.9 1.9 copy-start.5
  154.2 13.2 %collective-permute-start.21 = (bf16[256,256]{0,1:T(8,128)(2,1)S(1)}, bf16[256,256]{0,1:T(8,128)(2,1)S(1)}, u32[]{:S(2)}, u32[]{:S(2)}) collective-permute-start(bf16[256,256]{0,1:T(8,128)(2,1)S(1)} %bitcast.309), channel_id=1, source_target_pairs={{0,16},{4,20},{8,24},{12,28},{16,0},{20,4},{24,8},{28,12},{32,48},... | collective-permute-start | bytes 393224 | tf_op jit(solution)/shard_map/ppermute | solution.py:19
  160.0 25.8 %collective-permute-start.14 = (bf16[128,256]{1,0:T(8,128)(2,1)S(1)}, bf16[128,256]{1,0:T(8,128)(2,1)}, u32[]{:S(2)}, u32[]{:S(2)}) collective-permute-start(bf16[128,256]{1,0:T(8,128)(2,1)S(1)} %select_convert_fusion.5), channel_id=1, source_target_pairs={{0,4},{4,0},{8,12},{12,8},{16,20},{20,16},{24,28},{28,24},{32,36},... | collective-permute-start | bytes 196616 | tf_op jit(solution)/shard_map/ppermute | solution.py:19
  164.5 22.8 %collective-permute-start.20 = (bf16[128,256]{1,0:T(8,128)(2,1)S(1)}, bf16[128,256]{1,0:T(8,128)(2,1)}, u32[]{:S(2)}, u32[]{:S(2)}) collective-permute-start(bf16[128,256]{1,0:T(8,128)(2,1)S(1)} %select_convert_fusion.2), channel_id=1, source_target_pairs={{0,4},{4,0},{8,12},{12,8},{16,20},{20,16},{24,28},{28,24},{32,36},... | collective-permute-start | bytes 196616 | tf_op jit(solution)/shard_map/ppermute | solution.py:19
  167.4 5.0 %collective-permute-start.16 = (bf16[128,256]{0,1:T(8,128)(2,1)S(1)}, bf16[128,256]{0,1:T(8,128)(2,1)S(1)}, u32[]{:S(2)}, u32[]{:S(2)}) collective-permute-start(bf16[128,256]{0,1:T(8,128)(2,1)S(1)} %select_convert_fusion.4), channel_id=1, source_target_pairs={{0,8},{4,12},{8,0},{12,4},{16,24},{20,28},{24,16},{28,20},{32,40},... | collective-permute-start | bytes 196616 | tf_op jit(solution)/shard_map/ppermute | solution.py:19
  172.4 5.0 %collective-permute-start.22 = (bf16[128,256]{0,1:T(8,128)(2,1)S(1)}, bf16[128,256]{0,1:T(8,128)(2,1)S(1)}, u32[]{:S(2)}, u32[]{:S(2)}) collective-permute-start(bf16[128,256]{0,1:T(8,128)(2,1)S(1)} %select_convert_fusion.1), channel_id=1, source_target_pairs={{0,8},{4,12},{8,0},{12,4},{16,24},{20,28},{24,16},{28,20},{32,40},... | collective-permute-start | bytes 196616 | tf_op jit(solution)/shard_map/ppermute | solution.py:19
  177.4 5.6 %collective-permute-start.17 = (bf16[64,256]{0,1:T(8,128)(2,1)S(1)}, bf16[64,256]{0,1:T(8,128)(2,1)S(1)}, u32[]{:S(2)}, u32[]{:S(2)}) collective-permute-start(bf16[64,256]{0,1:T(8,128)(2,1)S(1)} %select_convert_fusion.3), channel_id=1, source_target_pairs={{0,4},{4,0},{8,12},{12,8},{16,20},{20,16},{24,28},{28,24},{32,36},... | collective-permute-start | bytes 98312 | tf_op jit(solution)/shard_map/ppermute | solution.py:19
  182.9 3.7 %collective-permute-start.23 = (bf16[64,256]{0,1:T(8,128)(2,1)S(1)}, bf16[64,256]{0,1:T(8,128)(2,1)S(1)}, u32[]{:S(2)}, u32[]{:S(2)}) collective-permute-start(bf16[64,256]{0,1:T(8,128)(2,1)S(1)} %select_convert_fusion), channel_id=1, source_target_pairs={{0,4},{4,0},{8,12},{12,8},{16,20},{20,16},{24,28},{28,24},{32,36},... | collective-permute-start | bytes 98312 | tf_op jit(solution)/shard_map/ppermute | solution.py:19
  (5 other events, 3.4 us)
where the time goes:
time: 196 us; the launch traced here: 193 us
  starting transfers between devices  71.3 us (36%)
  local copies, waits for them, and re-layouts  52.5 us (27%)
  matrix products  27.9 us (14%)
  other arithmetic  25.6 us (13%)
  waiting for transfers between devices  7.54 us (4%)
  blocking collectives  6.73 us (3%)
    ppermute x24, starting transfers between devices, swapped(): return lax.ppermute(value, axis, pairs)  71.3 us
    unnamed x96, local copies, waits for them, and re-layouts  9.7 us
    ppermute x24, waiting for transfers between devices, swapped(): return lax.ppermute(value, axis, pairs)  7.54 us
    psum x1, blocking collectives, on_device(): square = lax.psum(jnp.sum(out_float * out_float, axis=1), 'head')  6.73 us
    reshape x3, local copies, waits for them, and re-layouts, on_device(): attn_acc = attn_acc + jnp.einsum('ghrl,glhd->grhd', weight, value_view, p...  6.11 us
    ppermute x6, local copies, waits for them, and re-layouts, swapped(): return lax.ppermute(value, axis, pairs)  5.96 us
    dot_general x5, matrix products, on_device(): jnp.einsum('ghrl,glhd->grhd', weight, value_view, preferred_element_type=...  5.52 us
    dot_general x5, matrix products, on_device(): jnp.einsum('ghrl,glhd->grhd', dscore, key_view, preferred_element_type=jn...  5.4 us
  transfers between devices with their start and end apart: 24, of which 4 were waited for; matrix products, arithmetic and copies ran while one was open for 25% of the time, Pallas kernels for 0%

commit v1 on v0

v1 whole, which is shorter than its diff:
```python
import functools

import jax
import jax.numpy as jnp
from jax import lax
from jax.experimental import pallas as pl
from jax.experimental.pallas import tpu as pltpu
from jax.sharding import PartitionSpec as P

HEADS = 8
LEAF = 256
NORM_EPS = 1e-06

FAR = {1: (0, 256), 2: (256, 128), 3: (384, 128), 4: (512, 64), 5: (576, 64), 6: (640, 64), 7: (704, 64)}
OWN = {1: (0, 256), 2: (256, 128), 3: (256, 128), 4: (384, 64), 5: (384, 64), 6: (384, 64), 7: (384, 64)}
LOG2E = 1.4426950408889634

NT = (((1,), (1,)), ((), ()))
NN = (((1,), (0,)), ((), ()))


def mm(a, b, dims=NN):
    return lax.dot_general(a, b, dims, preferred_element_type=jnp.float32)


def flipped(position, number):
    for bit in (1, 2, 4):
        if number & bit:
            position = position + bit - 2 * bit * ((position // bit) % 2)
    return position


def kernel(
    q_hbm, k_hbm, v_hbm, gain_ref, co_hbm,
    norm_hbm, dq_hbm, dk_hbm, dv_hbm,
    q, kv, co, coarse, cot_out, cot_in, kvt, pt, gcot, gaint, ot, gb, dqt, stats, stats_in,
    dk_acc, dv_acc, out_buf,
    in_sem, out_sem, fs, fr, bs, br, ss, sr,
):
    rows, width = q.shape
    heads = 2
    hd = 128
    full = HEADS * hd
    scale = hd ** (-0.5)
    me_seq = lax.axis_index("seq")
    me_head = lax.axis_index("head")
    n_head = 4

    loads = [
        pltpu.make_async_copy(k_hbm, kv.at[pl.ds(0, rows), pl.ds(0, width)], in_sem.at[0]),
        pltpu.make_async_copy(v_hbm, kv.at[pl.ds(0, rows), pl.ds(width, width)], in_sem.at[1]),
        pltpu.make_async_copy(q_hbm, q, in_sem.at[2]),
        pltpu.make_async_copy(co_hbm, co, in_sem.at[3]),
    ]
    for load in loads:
        load.start()

    seq_peer = {j: {"seq": flipped(me_seq, j)} for j in FAR}
    head_peer = {j: {"head": (me_head + j) % n_head} for j in (1, 2, 3)}
    barrier = pltpu.get_barrier_semaphore()
    for peer in list(seq_peer.values()) + list(head_peer.values()):
        pl.semaphore_signal(barrier, inc=1, device_id=peer, device_id_type=pl.DeviceIdType.MESH)

    r = lax.broadcasted_iota(jnp.int32, (448, rows), 0)
    c = lax.broadcasted_iota(jnp.int32, (448, rows), 1)
    low = jnp.where(r < 256, 2 * r, jnp.where(r < 384, 4 * (r - 256), 8 * (r - 384)))
    size = jnp.where(r < 256, 2, jnp.where(r < 384, 4, 8))
    weight = jnp.where(r < 256, 0.5, jnp.where(r < 384, 0.25, 0.125))
    averages = jnp.where((c >= low) & (c < low + size), weight, 0.0).astype(jnp.bfloat16)
    loads[0].wait()
    loads[1].wait()
    coarse[...] = mm(averages, kv[0:rows, :]).astype(jnp.bfloat16)

    pl.semaphore_wait(barrier, len(seq_peer) + len(head_peer))
    forward = {}
    for j in (6, 7, 4, 5, 2, 3, 1):
        (own_row, count), (far_row, _) = OWN[j], FAR[j]
        forward[j] = pltpu.make_async_remote_copy(
            src_ref=coarse.at[pl.ds(own_row, count)],
            dst_ref=kv.at[pl.ds(rows + far_row, count)],
            send_sem=fs.at[j - 1],
            recv_sem=fr.at[j - 1],
            device_id=seq_peer[j],
            device_id_type=pl.DeviceIdType.MESH,
        )
        forward[j].start()

    loads[2].wait()

    def transposed_rows(at, count):
        kvt[:, at : at + count] = kv[at : at + count, :].T

    blocks = [(0, 512), (512, 256), (768, 256), (1024, 256)]
    half = rows // 2
    m_run = {}
    l_run = {}
    m_used = {}

    def forward_block(number, h, qh):
        at, count = blocks[number]
        q_cols = slice(qh * half, (qh + 1) * half)
        q_h = q[q_cols, h * hd : (h + 1) * hd]
        s = mm(kv[at : at + count, h * hd : (h + 1) * hd], q_h, NT) * (scale * LOG2E)
        top = jnp.max(s, axis=0, keepdims=True)
        if number > 0:
            top = jnp.maximum(top, m_run[h, qh])
        p = jnp.exp2(s - top)
        total = jnp.sum(p, axis=0, keepdims=True)
        p = p.astype(jnp.bfloat16)
        pt[h, at : at + count, q_cols] = p
        o = mm(kvt[width + h * hd : width + (h + 1) * hd, at : at + count], p)
        if number > 0:
            alpha = jnp.exp2(m_run[h, qh] - top)
            total = total + l_run[h, qh] * alpha
            o = o + ot[h * hd : (h + 1) * hd, q_cols] * alpha
        ot[h * hd : (h + 1) * hd, q_cols] = o
        m_run[h, qh] = top
        l_run[h, qh] = total
        m_used[number, h, qh] = top

    transposed_rows(0, 512)
    for h in range(heads):
        for qh in range(2):
            forward_block(0, h, qh)

    loads[3].wait()
    gain = gain_ref[...]
    for h in range(heads):
        cols = slice(h * hd, (h + 1) * hd)
        gaint[cols, :] = jnp.broadcast_to(gain[:, cols], (hd, hd)).T
        gcot[cols, :] = (co[:, cols].astype(jnp.float32) * gain[:, cols]).T

    forward[1].wait_recv()
    transposed_rows(512, 256)
    for h in range(heads):
        for qh in range(2):
            forward_block(1, h, qh)
    forward[2].wait_recv()
    forward[3].wait_recv()
    transposed_rows(768, 256)
    for h in range(heads):
        for qh in range(2):
            forward_block(2, h, qh)
    for j in (4, 5, 6, 7):
        forward[j].wait_recv()
    transposed_rows(1024, 256)

    lse = {}
    stat_copies = {}
    for qh in range(2):
        q_cols = slice(qh * half, (qh + 1) * half)
        square = jnp.zeros((1, half), jnp.float32)
        inner = jnp.zeros((1, half), jnp.float32)
        for h in range(heads):
            f = slice(h * hd, (h + 1) * hd)
            forward_block(3, h, qh)
            lse[h, qh] = m_run[h, qh] + jnp.log2(l_run[h, qh])
            o = (ot[f, q_cols] * (1.0 / l_run[h, qh])).astype(jnp.bfloat16).astype(jnp.float32)
            ot[f, q_cols] = o
            square = square + jnp.sum(o * o, axis=0, keepdims=True)
            inner = inner + jnp.sum(o * gcot[f, q_cols], axis=0, keepdims=True)
        for part in range(2):
            lanes = slice(part * 128, (part + 1) * 128)
            stats[qh, part : part + 1, :] = square[:, lanes]
            stats[qh, 2 + part : 3 + part, :] = inner[:, lanes]
        for j in (1, 2, 3):
            copy = pltpu.make_async_remote_copy(
                src_ref=stats.at[qh],
                dst_ref=stats_in.at[qh, j - 1],
                send_sem=ss.at[qh, j - 1],
                recv_sem=sr.at[qh, j - 1],
                device_id=head_peer[j],
                device_id_type=pl.DeviceIdType.MESH,
            )
            copy.start()
            stat_copies[qh, j] = copy

    delta = {}
    for qh in range(2):
        q_cols = slice(qh * half, (qh + 1) * half)
        for j in (1, 2, 3):
            stat_copies[qh, j].wait_recv()
        both = stats[qh] + stats_in[qh, 0] + stats_in[qh, 1] + stats_in[qh, 2]
        square = jnp.concatenate([both[0:1], both[1:2]], axis=1)
        inner = jnp.concatenate([both[2:3], both[3:4]], axis=1)
        inverse = lax.rsqrt(square * (1.0 / full) + NORM_EPS)
        slope = inverse * inverse * inverse * inner * (1.0 / full)
        for h in range(heads):
            f = slice(h * hd, (h + 1) * hd)
            o = ot[f, q_cols]
            gain_col = gaint[f, :]
            normed = o * inverse * jnp.concatenate([gain_col] * (half // 128), axis=1)
            out_buf[0, q_cols, f] = normed.T.astype(jnp.bfloat16)
            g = (gcot[f, q_cols] * inverse - o * slope).astype(jnp.bfloat16).astype(jnp.float32)
            delta[h, qh] = jnp.sum(g * o, axis=0, keepdims=True)
            for number in range(4):
                e = jnp.exp2(m_used[number, h, qh] - lse[h, qh])
                gb[number, f, q_cols] = (g * e).astype(jnp.bfloat16)
                delta[number, h, qh] = delta[h, qh] * e
    stores = [pltpu.make_async_copy(out_buf.at[i], ref, out_sem.at[i]) for i, ref in enumerate((norm_hbm, dq_hbm, dk_hbm, dv_hbm))]
    stores[0].start()

    def backward_block(number, h):
        at, count = blocks[number]
        f = slice(h * hd, (h + 1) * hd)
        fv = slice(width + h * hd, width + (h + 1) * hd)
        g = gb[number, f, :]
        p = pt[h, at : at + count, :]
        d_row = jnp.concatenate([delta[number, h, 0], delta[number, h, 1]], axis=1)
        dp = mm(kv[at : at + count, fv], g)
        ds = (p.astype(jnp.float32) * (dp - d_row)).astype(jnp.bfloat16)
        dv = mm(p, g, NT)
        dk = mm(ds, q[:, f]) * scale
        dq = mm(kvt[f, at : at + count], ds)
        if number == 3:
            dqt[f, :] = dq
        else:
            dqt[f, :] = dqt[f, :] + dq
        if number == 0:
            dk_acc[:, f] = dk
            dv_acc[:, f] = dv
        else:
            cot_out[at - rows : at - rows + count, f] = dk.astype(jnp.bfloat16)
            cot_out[at - rows : at - rows + count, fv] = dv.astype(jnp.bfloat16)

    backward = {}

    def send_back(j):
        far_row, count = FAR[j]
        backward[j] = pltpu.make_async_remote_copy(
            src_ref=cot_out.at[pl.ds(far_row, count)],
            dst_ref=cot_in.at[pl.ds(far_row, count)],
            send_sem=bs.at[j - 1],
            recv_sem=br.at[j - 1],
            device_id=seq_peer[j],
            device_id_type=pl.DeviceIdType.MESH,
        )
        backward[j].start()

    for number, partners in ((3, (6, 7, 4, 5)), (2, (2, 3)), (1, (1,))):
        for h in range(heads):
            backward_block(number, h)
        for j in partners:
            send_back(j)
    for h in range(heads):
        backward_block(0, h)
        f = slice(h * hd, (h + 1) * hd)
        out_buf[1, :, f] = (dqt[f, :] * scale).T.astype(jnp.bfloat16)
    stores[1].start()

    def spread(count, by):
        r = lax.broadcasted_iota(jnp.int32, (rows, count), 0)
        c = lax.broadcasted_iota(jnp.int32, (rows, count), 1)
        c = c % (rows // by)
        return jnp.where((r >= by * c) & (r < by * (c + 1)), 1.0 / by, 0.0).astype(jnp.bfloat16)

    for at, by, partners in ((0, 2, (1,)), (256, 4, (2, 3)), (512, 8, (4, 5, 6, 7))):
        matrix = spread(256, by)
        for j in partners:
            backward[j].wait_recv()
        added = mm(matrix, cot_in[at : at + 256, :])
        if by < 8:
            dk_acc[...] = dk_acc[...] + added[:, :width]
            dv_acc[...] = dv_acc[...] + added[:, width:]
        else:
            out_buf[2] = (dk_acc[...] + added[:, :width]).astype(jnp.bfloat16)
            stores[2].start()
            out_buf[3] = (dv_acc[...] + added[:, width:]).astype(jnp.bfloat16)
            stores[3].start()

    for copy in list(forward.values()) + list(backward.values()) + list(stat_copies.values()):
        copy.wait_send()
    for store in stores:
        store.wait()


def on_device(queries, key_tokens, value_tokens, norm_gain, out_cotangent):
    rows, width = queries.shape
    out = jax.ShapeDtypeStruct((rows, width), jnp.bfloat16)
    bf, f32 = jnp.bfloat16, jnp.float32
    anywhere = pl.BlockSpec(memory_space=pl.ANY)
    dma = pltpu.SemaphoreType.DMA
    return pl.pallas_call(
        kernel,
        out_shape=(out, out, out, out),
        in_specs=[anywhere, anywhere, anywhere, pl.BlockSpec(memory_space=pltpu.VMEM), anywhere],
        out_specs=(anywhere,) * 4,
        scratch_shapes=[
            pltpu.VMEM((rows, width), bf),
            pltpu.VMEM((rows + 768, 2 * width), bf),
            pltpu.VMEM((rows, width), bf),
            pltpu.VMEM((448, 2 * width), bf),
            pltpu.VMEM((768, 2 * width), bf),
            pltpu.VMEM((768, 2 * width), bf),
            pltpu.VMEM((2 * width, rows + 768), bf),
            pltpu.VMEM((2, rows + 768, rows), bf),
            pltpu.VMEM((width, rows), f32),
            pltpu.VMEM((width, 128), f32),
            pltpu.VMEM((width, rows), f32),
            pltpu.VMEM((4, width, rows), bf),
            pltpu.VMEM((width, rows), f32),
            pltpu.VMEM((2, 8, 128), f32),
            pltpu.VMEM((2, 3, 8, 128), f32),
            pltpu.VMEM((rows, width), f32),
            pltpu.VMEM((rows, width), f32),
            pltpu.VMEM((4, rows, width), bf),
            dma((4,)), dma((4,)), dma((7,)), dma((7,)), dma((7,)), dma((7,)), dma((2, 3)), dma((2, 3)),
        ],
        compiler_params=pltpu.CompilerParams(
            collective_id=0, has_side_effects=True, vmem_limit_bytes=48 * 2**20
        ),
    )(queries, key_tokens, value_tokens, norm_gain.reshape(1, width), out_cotangent)


def solution(mesh):
    return jax.shard_map(
        on_device,
        mesh=mesh,
        in_specs=(P("seq", "head"), P("seq", "head"), P("seq", "head"), P("head"), P("seq", "head")),
        out_specs=(P("seq", "head"),) * 4,
        check_vma=False,
    )
```

time: 196 us -> 47.9 us (0.24); the launches traced: 193 us -> 47.6 us
  starting transfers between devices: 71.3 us -> 0 us
  local copies, waits for them, and re-layouts: 52.5 us -> 7.28 us
  Pallas kernels: 0 us -> 39.7 us
  matrix products: 27.9 us -> 0 us
  other arithmetic: 25.6 us -> 0 us
  waiting for transfers between devices: 7.54 us -> 0 us
  blocking collectives: 6.73 us -> 0 us
    ppermute x24 -> x0, starting transfers between devices: 71.3 us -> none  [swapped(): return lax.ppermute(value, axis, pairs)]
    pallas_call x0 -> x1, Pallas kernels: none -> 39.7 us  [on_device(): pl.pallas_call(kernel, out_shape=(out, out, out, out), in_specs=[anywhere...]
    dot_general x30 -> x0, matrix products: 27.9 us -> none  [the longest x5 5.52 us: on_device(): jnp.einsum('ghrl,glhd->grhd', weight, value_view, preferred_element_type=...]
    reshape x18 -> x0, local copies, waits for them, and re-layouts: 15.2 us -> none  [the longest x3 6.11 us: on_device(): attn_acc = attn_acc + jnp.einsum('ghrl,glhd->grhd', weight, value_view, p...]
    convert_element_type x18 -> x0, other arithmetic: 9 us -> none  [the longest x4 2.87 us: halve_rows(): coarse.astype(jnp.float32).reshape((row_count // 2, 2) + coarse.shape[1:])]
    ppermute x24 -> x0, waiting for transfers between devices: 7.54 us -> none  [swapped(): return lax.ppermute(value, axis, pairs)]
    psum x1 -> x0, blocking collectives: 6.73 us -> none  [on_device(): square = lax.psum(jnp.sum(out_float * out_float, axis=1), 'head')]
    ppermute x6 -> x0, local copies, waits for them, and re-layouts: 5.96 us -> none  [swapped(): return lax.ppermute(value, axis, pairs)]
  transfers between devices with their start and end apart: 24 -> 0, of which waited for: 4 -> 0; matrix products, arithmetic and copies ran while one was open for 25% -> 0% of each run, Pallas kernels for 0% -> 0%
where the time goes in v1:
time: 47.9 us; the launch traced here: 47.6 us
  Pallas kernels  39.7 us (83%)
  local copies, waits for them, and re-layouts  7.28 us (15%)
  between operations  0.65 us (1%)
    pallas_call x1, Pallas kernels, on_device(): pl.pallas_call(kernel, out_shape=(out, out, out, out), in_specs=[anywhere...  39.7 us
    unnamed x14, local copies, waits for them, and re-layouts  7.28 us

profile of v1, /device:TPU:1, one launch (start us, length us, event | category | flops | bytes accessed | tf_op | source)
XLA Modules:
  0.0 47.6 jit_solution(8651809172772635369)
XLA Ops:
  0.6 0.0 copy-start.4
  0.6 0.7 %copy-done.4 = f32[256]{0:T(256)S(1)} copy-done((f32[256]{0:T(256)S(1)}, f32[256]{0:T(256)}, u32[]{:S(2)}) %copy-start.4) | copy-done | bytes 1048
  1.3 0.0 copy-start
  1.3 0.9 %copy-done = bf16[512,256]{1,0:T(8,128)(2,1)S(1)} copy-done((bf16[512,256]{1,0:T(8,128)(2,1)S(1)}, bf16[512,256]{1,0:T(8,128)(2,1)}, u32[]{:S(2)}) %copy-start) | copy-done | bytes 262168
  2.3 0.0 copy-start.1
  2.3 0.9 %copy-done.1 = bf16[512,256]{1,0:T(8,128)(2,1)S(1)} copy-done((bf16[512,256]{1,0:T(8,128)(2,1)S(1)}, bf16[512,256]{1,0:T(8,128)(2,1)}, u32[]{:S(2)}) %copy-start.1) | copy-done | bytes 262168
  3.2 0.0 copy-start.2
  3.2 0.9 %copy-done.2 = bf16[512,256]{1,0:T(8,128)(2,1)S(1)} copy-done((bf16[512,256]{1,0:T(8,128)(2,1)S(1)}, bf16[512,256]{1,0:T(8,128)(2,1)}, u32[]{:S(2)}) %copy-start.2) | copy-done | bytes 262168
  4.2 0.0 copy-start.3
  4.2 0.9 %copy-done.3 = bf16[512,256]{1,0:T(8,128)(2,1)S(1)} copy-done((bf16[512,256]{1,0:T(8,128)(2,1)S(1)}, bf16[512,256]{1,0:T(8,128)(2,1)}, u32[]{:S(2)}) %copy-start.3) | copy-done | bytes 262168
  5.1 39.7 %shard_map.84 = (bf16[512,256]{1,0:T(8,128)(2,1)S(1)}, bf16[512,256]{1,0:T(8,128)(2,1)S(1)}, bf16[512,256]{1,0:T(8,128)(2,1)S(1)}, bf16[512,256]{1,0:T(8,128)(2,1)S(1)}) custom-call(bf16[512,256]{1,0:T(8,128)(2,1)S(1)} %copy-done, bf16[512,256]{1,0:T(8,128)(2,1)S(1)} %copy-done.1, bf16[512,256]{1,0:T(8,128)(2,1)S(1)} %copy-done.2, f32[1,256]{1,0:T(1,128)S(1)} %bitcast.1, ...), custom_call_target="tpu_custom_call" | custom-call | tf_op jit(solution)/shard_map/pallas_call | solution.py:283
  44.8 0.7 %copy.13 = bf16[512,256]{1,0:T(8,128)(2,1)} copy(bf16[512,256]{1,0:T(8,128)(2,1)S(1)} %get-tuple-element.8) | data formatting | bytes 524288
  45.5 0.7 %copy.14 = bf16[512,256]{1,0:T(8,128)(2,1)} copy(bf16[512,256]{1,0:T(8,128)(2,1)S(1)} %get-tuple-element.9) | data formatting | bytes 524288
  46.2 0.7 %copy.15 = bf16[512,256]{1,0:T(8,128)(2,1)} copy(bf16[512,256]{1,0:T(8,128)(2,1)S(1)} %get-tuple-element.10) | data formatting | bytes 524288
  46.9 0.7 %copy.16 = bf16[512,256]{1,0:T(8,128)(2,1)} copy(bf16[512,256]{1,0:T(8,128)(2,1)S(1)} %get-tuple-element.11) | data formatting | bytes 524288
Async XLA Ops:
  0.6 0.7 %copy-start.4 = (f32[256]{0:T(256)S(1)}, f32[256]{0:T(256)}, u32[]{:S(2)}) copy-start(f32[256]{0:T(256)} %param.8) | copy-start | bytes 3076
  1.3 0.9 %copy-start = (bf16[512,256]{1,0:T(8,128)(2,1)S(1)}, bf16[512,256]{1,0:T(8,128)(2,1)}, u32[]{:S(2)}) copy-start(bf16[512,256]{1,0:T(8,128)(2,1)} %q_hbm.1) | copy-start | bytes 786436
  2.3 0.9 %copy-start.1 = (bf16[512,256]{1,0:T(8,128)(2,1)S(1)}, bf16[512,256]{1,0:T(8,128)(2,1)}, u32[]{:S(2)}) copy-start(bf16[512,256]{1,0:T(8,128)(2,1)} %k_hbm.1) | copy-start | bytes 786436
  3.2 0.9 %copy-start.2 = (bf16[512,256]{1,0:T(8,128)(2,1)S(1)}, bf16[512,256]{1,0:T(8,128)(2,1)}, u32[]{:S(2)}) copy-start(bf16[512,256]{1,0:T(8,128)(2,1)} %v_hbm.1) | copy-start | bytes 786436
  4.2 0.9 %copy-start.3 = (bf16[512,256]{1,0:T(8,128)(2,1)S(1)}, bf16[512,256]{1,0:T(8,128)(2,1)}, u32[]{:S(2)}) copy-start(bf16[512,256]{1,0:T(8,128)(2,1)} %co_hbm.1) | copy-start | bytes 786436

commit v2 on v1

v2 whole, which is shorter than its diff:
```python
import functools

import jax
import jax.numpy as jnp
from jax import lax
from jax.experimental import pallas as pl
from jax.experimental.pallas import tpu as pltpu
from jax.sharding import PartitionSpec as P

HEADS = 8
NORM_EPS = 1e-06
LOG2E = 1.4426950408889634

LOCAL, TWIN, DIRECT, HANDED = (0, 512), (512, 256), (768, 256), (1024, 256)
LINKED = {6: (192, 64, 384), 4: (128, 64, 384), 2: (0, 128, 256)}

NT = (((1,), (1,)), ((), ()))
NN = (((1,), (0,)), ((), ()))


def mm(a, b, dims=NN):
    return lax.dot_general(a, b, dims, preferred_element_type=jnp.float32)


def flipped(position, number):
    for bit in (1, 2, 4):
        if number & bit:
            position = position + bit - 2 * bit * ((position // bit) % 2)
    return position


def kernel(
    q_hbm, k_hbm, v_hbm, gain_hbm, co_hbm,
    norm_out, dq_out, dk_out, dv_out,
    q, kv, co, gain_ref, coarse, cot_out, cot_sib, cot_send, cot_in, kvt, pt, gcot, gaint, ot, gb, dqt, stats, stats_in,
    acc,
    in_sem, fs, fr, bs, br, ss, sr,
):
    rows, width = q.shape
    hd = 128
    heads = width // hd
    full = HEADS * hd
    scale = hd ** (-0.5)
    half = rows // 2
    me_seq = lax.axis_index("seq")
    me_head = lax.axis_index("head")
    n_head = HEADS // heads

    kv_loads = []
    for h in range(heads):
        for i, ref in enumerate((k_hbm, v_hbm)):
            kv_loads.append(
                pltpu.make_async_copy(
                    ref.at[:, pl.ds(h * hd, hd)],
                    kv.at[h, pl.ds(0, rows), pl.ds(i * hd, hd)],
                    in_sem.at[2 * h + i],
                )
            )
    q_load = pltpu.make_async_copy(q_hbm, q, in_sem.at[4])
    co_load = pltpu.make_async_copy(co_hbm, co, in_sem.at[5])
    gain_load = pltpu.make_async_copy(gain_hbm, gain_ref, in_sem.at[6])
    for load in kv_loads + [q_load, co_load, gain_load]:
        load.start()

    seq_peer = {j: {"seq": flipped(me_seq, j)} for j in (1, 2, 4, 6)}
    head_peer = {j: {"head": (me_head + j) % n_head} for j in (1, 2, 3)}
    barrier = pltpu.get_barrier_semaphore()
    for peer in list(seq_peer.values()) + list(head_peer.values()):
        pl.semaphore_signal(barrier, inc=1, device_id=peer, device_id_type=pl.DeviceIdType.MESH)

    sent = []

    def send(src, dst, send_sem, recv_sem, peer):
        copy = pltpu.make_async_remote_copy(
            src_ref=src, dst_ref=dst, send_sem=send_sem, recv_sem=recv_sem,
            device_id=peer, device_id_type=pl.DeviceIdType.MESH,
        )
        copy.start()
        sent.append(copy)
        return copy

    r = lax.broadcasted_iota(jnp.int32, (448, rows), 0)
    c = lax.broadcasted_iota(jnp.int32, (448, rows), 1)
    low = jnp.where(r < 256, 2 * r, jnp.where(r < 384, 4 * (r - 256), 8 * (r - 384)))
    size = jnp.where(r < 256, 2, jnp.where(r < 384, 4, 8))
    weight = jnp.where(r < 256, 0.5, jnp.where(r < 384, 0.25, 0.125))
    averages = jnp.where((c >= low) & (c < low + size), weight, 0.0).astype(jnp.bfloat16)

    linked = {}
    twin = {}
    for h in range(heads):
        kv_loads[2 * h].wait()
        kv_loads[2 * h + 1].wait()
        coarse[h] = mm(averages, kv[h, 0:rows, :]).astype(jnp.bfloat16)
        if h == 0:
            pl.semaphore_wait(barrier, len(seq_peer) + len(head_peer))
        for i, (j, (at, count, own)) in enumerate(LINKED.items()):
            linked[h, j] = send(
                coarse.at[h, pl.ds(own, count)], kv.at[h, pl.ds(DIRECT[0] + at, count)],
                fs.at[h, i], fr.at[h, i], seq_peer[j],
            )
        twin[h] = send(
            coarse.at[h, pl.ds(0, 256)], kv.at[h, pl.ds(TWIN[0], 256)], fs.at[h, 3], fr.at[h, 3], seq_peer[1]
        )
    handed = {}

    def hand_on(h):
        for j in LINKED:
            linked[h, j].wait_recv()
        handed[h] = send(
            kv.at[h, pl.ds(DIRECT[0], 256)], kv.at[h, pl.ds(HANDED[0], 256)], fs.at[h, 4], fr.at[h, 4], seq_peer[1]
        )

    def transposed_rows(h, block):
        at, count = block
        kvt[h, :, at : at + count] = kv[h, at : at + count, :].T

    m_run, l_run, m_used = {}, {}, {}

    def forward_block(block, h, qh):
        at, count = block
        q_cols = slice(qh * half, (qh + 1) * half)
        q_h = q[q_cols, h * hd : (h + 1) * hd]
        s = mm(kv[h, at : at + count, 0:hd], q_h, NT) * (scale * LOG2E)
        top = jnp.max(s, axis=0, keepdims=True)
        first = (h, qh) not in m_run
        if not first:
            top = jnp.maximum(top, m_run[h, qh])
        p = jnp.exp2(s - top)
        total = jnp.sum(p, axis=0, keepdims=True)
        p = p.astype(jnp.bfloat16)
        pt[h, at : at + count, q_cols] = p
        o = mm(kvt[h, hd : 2 * hd, at : at + count], p)
        if not first:
            alpha = jnp.exp2(m_run[h, qh] - top)
            total = total + l_run[h, qh] * alpha
            o = o + ot[h * hd : (h + 1) * hd, q_cols] * alpha
        ot[h * hd : (h + 1) * hd, q_cols] = o
        m_run[h, qh] = top
        l_run[h, qh] = total
        m_used[block, h, qh] = top

    q_load.wait()
    for h in range(heads):
        transposed_rows(h, LOCAL)
        for qh in range(2):
            forward_block(LOCAL, h, qh)
    for h in range(heads):
        twin[h].wait_recv()
        transposed_rows(h, TWIN)
        for qh in range(2):
            forward_block(TWIN, h, qh)

    co_load.wait()
    gain_load.wait()
    gain = gain_ref[...]
    for h in range(heads):
        f = slice(h * hd, (h + 1) * hd)
        gaint[f, :] = jnp.broadcast_to(gain[:, f], (hd, hd)).T
        gcot[f, :] = (co[:, f].astype(jnp.float32) * gain[:, f]).T

    hand_on(0)
    transposed_rows(0, DIRECT)
    for qh in range(2):
        forward_block(DIRECT, 0, qh)
    handed[0].wait_recv()
    transposed_rows(0, HANDED)
    for qh in range(2):
        forward_block(HANDED, 0, qh)
    hand_on(1)
    transposed_rows(1, DIRECT)
    for qh in range(2):
        forward_block(DIRECT, 1, qh)
    handed[1].wait_recv()
    transposed_rows(1, HANDED)

    lse = {}
    stat_copies = {}
    for qh in range(2):
        q_cols = slice(qh * half, (qh + 1) * half)
        square = jnp.zeros((1, half), jnp.float32)
        inner = jnp.zeros((1, half), jnp.float32)
        forward_block(HANDED, 1, qh)
        for h in range(heads):
            f = slice(h * hd, (h + 1) * hd)
            lse[h, qh] = m_run[h, qh] + jnp.log2(l_run[h, qh])
            o = (ot[f, q_cols] * (1.0 / l_run[h, qh])).astype(jnp.bfloat16).astype(jnp.float32)
            ot[f, q_cols] = o
            square = square + jnp.sum(o * o, axis=0, keepdims=True)
            inner = inner + jnp.sum(o * gcot[f, q_cols], axis=0, keepdims=True)
        for part in range(2):
            lanes = slice(part * 128, (part + 1) * 128)
            stats[qh, part : part + 1, :] = square[:, lanes]
            stats[qh, 2 + part : 3 + part, :] = inner[:, lanes]
        for j in (2, 1, 3):
            stat_copies[qh, j] = send(
                stats.at[qh], stats_in.at[qh, j - 1], ss.at[qh, j - 1], sr.at[qh, j - 1], head_peer[j]
            )

    delta = {}
    used = (LOCAL, TWIN, DIRECT, HANDED)
    for qh in range(2):
        q_cols = slice(qh * half, (qh + 1) * half)
        for j in (1, 2, 3):
            stat_copies[qh, j].wait_recv()
        both = stats[qh] + stats_in[qh, 0] + stats_in[qh, 1] + stats_in[qh, 2]
        square = jnp.concatenate([both[0:1], both[1:2]], axis=1)
        inner = jnp.concatenate([both[2:3], both[3:4]], axis=1)
        inverse = lax.rsqrt(square * (1.0 / full) + NORM_EPS)
        slope = inverse * inverse * inverse * inner * (1.0 / full)
        for h in range(heads):
            f = slice(h * hd, (h + 1) * hd)
            o = ot[f, q_cols]
            g = (gcot[f, q_cols] * inverse - o * slope).astype(jnp.bfloat16).astype(jnp.float32)
            whole = jnp.sum(g * o, axis=0, keepdims=True)
            for number, block in enumerate(used):
                e = jnp.exp2(m_used[block, h, qh] - lse[h, qh])
                gb[number, f, q_cols] = (g * e).astype(jnp.bfloat16)
                delta[block, h, qh] = whole * e
            gcot[f, q_cols] = o * inverse * jnp.concatenate([gaint[f, :]] * (half // 128), axis=1)

    def backward_block(block, h):
        at, count = block
        f = slice(h * hd, (h + 1) * hd)
        g = gb[used.index(block), f, :]
        p = pt[h, at : at + count, :]
        d_row = jnp.concatenate([delta[block, h, 0], delta[block, h, 1]], axis=1)
        dp = mm(kv[h, at : at + count, hd : 2 * hd], g)
        ds = (p.astype(jnp.float32) * (dp - d_row)).astype(jnp.bfloat16)
        dv = mm(p, g, NT)
        dk = mm(ds, q[:, f]) * scale
        dq = mm(kvt[h, 0:hd, at : at + count], ds)
        if block == HANDED:
            dqt[f, :] = dq
        else:
            dqt[f, :] = dqt[f, :] + dq
        if block == LOCAL:
            acc[h, :, 0:hd] = dk
            acc[h, :, hd : 2 * hd] = dv
        else:
            to = at - rows
            cot_out[h, to : to + count, 0:hd] = dk.astype(jnp.bfloat16)
            cot_out[h, to : to + count, hd : 2 * hd] = dv.astype(jnp.bfloat16)

    sib, back, back_twin = {}, {}, {}

    def send_back(h):
        sib[h].wait_recv()
        mine = cot_out[h, 256:512, :].astype(jnp.float32)
        cot_send[h] = (mine + cot_sib[h].astype(jnp.float32)).astype(jnp.bfloat16)
        for i, (j, (at, count, _)) in enumerate(LINKED.items()):
            back[h, j] = send(
                cot_send.at[h, pl.ds(at, count)], cot_in.at[h, pl.ds(256 + at, count)],
                bs.at[h, i], br.at[h, i], seq_peer[j],
            )

    for h in range(heads):
        backward_block(HANDED, h)
        sib[h] = send(cot_out.at[h, pl.ds(512, 256)], cot_sib.at[h], bs.at[h, 4], br.at[h, 4], seq_peer[1])
        if h > 0:
            send_back(h - 1)
        backward_block(DIRECT, h)
    send_back(heads - 1)
    for h in range(heads):
        backward_block(TWIN, h)
        back_twin[h] = send(
            cot_out.at[h, pl.ds(0, 256)], cot_in.at[h, pl.ds(0, 256)], bs.at[h, 3], br.at[h, 3], seq_peer[1]
        )
    for h in range(heads):
        f = slice(h * hd, (h + 1) * hd)
        backward_block(LOCAL, h)
        dq_out[:, f] = (dqt[f, :] * scale).T.astype(jnp.bfloat16)
        norm_out[:, f] = gcot[f, :].T.astype(jnp.bfloat16)

    r = lax.broadcasted_iota(jnp.int32, (rows, 256), 0)
    c = lax.broadcasted_iota(jnp.int32, (rows, 256), 1)
    halves = jnp.where(r // 2 == c, 0.5, 0.0).astype(jnp.bfloat16)
    low = jnp.where(c < 128, 4 * c, 8 * ((c - 128) % 64))
    size = jnp.where(c < 128, 4, 8)
    weight = jnp.where(c < 128, 0.25, 0.125)
    others = jnp.where((r >= low) & (r < low + size), weight, 0.0).astype(jnp.bfloat16)
    for h in range(heads):
        back_twin[h].wait_recv()
        acc[h] = acc[h] + mm(halves, cot_in[h, 0:256, :])
    for h in range(heads):
        f = slice(h * hd, (h + 1) * hd)
        for j in LINKED:
            back[h, j].wait_recv()
        total = acc[h] + mm(others, cot_in[h, 256:512, :])
        dk_out[:, f] = total[:, 0:hd].astype(jnp.bfloat16)
        dv_out[:, f] = total[:, hd : 2 * hd].astype(jnp.bfloat16)

    for copy in sent:
        copy.wait_send()


def store_kernel(*refs):
    copies = [pltpu.make_async_copy(refs[i], refs[4 + i], refs[8].at[i]) for i in range(4)]
    for copy in copies:
        copy.start()
    for copy in copies:
        copy.wait()


def on_device(queries, key_tokens, value_tokens, norm_gain, out_cotangent):
    rows, width = queries.shape
    bf, f32 = jnp.bfloat16, jnp.float32
    hbm = pl.BlockSpec(memory_space=pltpu.HBM)
    vmem = pl.BlockSpec(memory_space=pltpu.VMEM)
    dma = pltpu.SemaphoreType.DMA
    in_hbm = functools.partial(pltpu.with_memory_space_constraint, memory_space=pltpu.HBM)
    in_vmem = functools.partial(pltpu.with_memory_space_constraint, memory_space=pltpu.VMEM)
    results = pl.pallas_call(
        kernel,
        out_shape=(pltpu.VMEM((rows, width), bf),) * 4,
        in_specs=[hbm] * 5,
        out_specs=(vmem,) * 4,
        scratch_shapes=[
            pltpu.VMEM((rows, width), bf),
            pltpu.VMEM((2, rows + 768, width), bf),
            pltpu.VMEM((rows, width), bf),
            pltpu.VMEM((1, width), f32),
            pltpu.VMEM((2, 448, width), bf),
            pltpu.VMEM((2, 768, width), bf),
            pltpu.VMEM((2, 256, width), bf),
            pltpu.VMEM((2, 256, width), bf),
            pltpu.VMEM((2, 512, width), bf),
            pltpu.VMEM((2, width, rows + 768), bf),
            pltpu.VMEM((2, rows + 768, rows), bf),
            pltpu.VMEM((width, rows), f32),
            pltpu.VMEM((width, 128), f32),
            pltpu.VMEM((width, rows), f32),
            pltpu.VMEM((4, width, rows), bf),
            pltpu.VMEM((width, rows), f32),
            pltpu.VMEM((2, 8, 128), f32),
            pltpu.VMEM((2, 3, 8, 128), f32),
            pltpu.VMEM((2, rows, width), f32),
            dma((7,)), dma((2, 5)), dma((2, 5)), dma((2, 5)), dma((2, 5)), dma((2, 3)), dma((2, 3)),
        ],
        compiler_params=pltpu.CompilerParams(
            collective_id=0, has_side_effects=True, vmem_limit_bytes=48 * 2**20
        ),
    )(in_hbm(queries), in_hbm(key_tokens), in_hbm(value_tokens), in_hbm(norm_gain.reshape(1, width)), in_hbm(out_cotangent))
    return pl.pallas_call(
        store_kernel,
        out_shape=(pltpu.HBM((rows, width), bf),) * 4,
        in_specs=[vmem] * 4,
        out_specs=(hbm,) * 4,
        scratch_shapes=[dma((4,))],
    )(*[in_vmem(result) for result in results])


def solution(mesh):
    return jax.shard_map(
        on_device,
        mesh=mesh,
        in_specs=(P("seq", "head"), P("seq", "head"), P("seq", "head"), P("head"), P("seq", "head")),
        out_specs=(P("seq", "head"),) * 4,
        check_vma=False,
    )
```

time: 47.9 us -> 32.2 us (0.67)
  Pallas kernels: 39.7 us -> 31.5 us
  local copies, waits for them, and re-layouts: 7.28 us -> 0 us
    pallas_call x1 -> x2, Pallas kernels: 39.7 us -> 31.5 us  [the longest x1 30.5 us: on_device(): pl.pallas_call(kernel, out_shape=(pltpu.VMEM((rows, width), bf),) * 4, in...]
    unnamed x14 -> x0, local copies, waits for them, and re-layouts: 7.28 us -> none
where the time goes in v2:
time: 32.2 us; the launch traced here: 32.1 us
  Pallas kernels  31.5 us (98%)
  between operations  0.64 us (2%)
    pallas_call x1, Pallas kernels, on_device(): pl.pallas_call(kernel, out_shape=(pltpu.VMEM((rows, width), bf),) * 4, in...  30.5 us
    pallas_call x1, Pallas kernels, on_device(): pl.pallas_call(store_kernel, out_shape=(pltpu.HBM((rows, width), bf),) *...  1 us

profile of v2, /device:TPU:1, one launch (start us, length us, event | category | flops | bytes accessed | tf_op | source)
XLA Modules:
  0.0 32.1 jit_solution(5735129972691593766)
XLA Ops:
  0.6 30.5 %shard_map.84 = (bf16[512,256]{1,0:T(8,128)(2,1)S(1)}, bf16[512,256]{1,0:T(8,128)(2,1)S(1)}, bf16[512,256]{1,0:T(8,128)(2,1)S(1)}, bf16[512,256]{1,0:T(8,128)(2,1)S(1)}) custom-call(bf16[512,256]{1,0:T(8,128)(2,1)} %q_hbm.1, bf16[512,256]{1,0:T(8,128)(2,1)} %k_hbm.1, bf16[512,256]{1,0:T(8,128)(2,1)} %v_hbm.1, f32[1,256]{1,0:T(1,128)} %bitcast.1, ...), custom_call_target="tpu_custom_call" | custom-call | tf_op jit(solution)/shard_map/pallas_call | solution.py:313
  31.1 1.0 %shard_map.85 = (bf16[512,256]{1,0:T(8,128)(2,1)}, bf16[512,256]{1,0:T(8,128)(2,1)}, bf16[512,256]{1,0:T(8,128)(2,1)}, bf16[512,256]{1,0:T(8,128)(2,1)}) custom-call(bf16[512,256]{1,0:T(8,128)(2,1)S(1)} %get-tuple-element.8.refs_0_, bf16[512,256]{1,0:T(8,128)(2,1)S(1)} %get-tuple-element.9.refs_1_, bf16[512,256]{1,0:T(8,128)(2,1)S(1)} %get-tuple-element.10.refs_2_, ...), custom_call_target="tpu_custom_call" | custom-call | tf_op jit(solution)/shard_map/pallas_call | solution.py:344

commit v3 on v2

v3 whole, which is shorter than its diff:
```python
import functools

import jax
import jax.numpy as jnp
from jax import lax
from jax.experimental import pallas as pl
from jax.experimental.pallas import tpu as pltpu
from jax.sharding import PartitionSpec as P

HEADS = 8
NORM_EPS = 1e-06
LOG2E = 1.4426950408889634

LOCAL, TWIN = (0, 512), (512, 256)
LINKED = {
    7: (448, 64, 384, 192), 6: (384, 64, 384, 192), 5: (320, 64, 384, 128), 4: (256, 64, 384, 128),
    3: (128, 128, 256, 0), 2: (0, 128, 256, 0),
}

NT = (((1,), (1,)), ((), ()))
NN = (((1,), (0,)), ((), ()))


def mm(a, b, dims=NN):
    return lax.dot_general(a, b, dims, preferred_element_type=jnp.float32)


def flipped(position, number):
    for bit in (1, 2, 4):
        if number & bit:
            position = position + bit - 2 * bit * ((position // bit) % 2)
    return position


def kernel(
    q_hbm, k_hbm, v_hbm, gain_hbm, co_hbm,
    norm_out, dq_out, dk_out, dv_out,
    near, far, near_t, far_t, given, qh, coh, gain_ref, coarse, cot_out, cot_in, pt, pf, gcot, ot, gb, dqt, stats, stats_in,
    acc, back_out, back_in, twin_cot,
    in_sem, fs, fr, bs, br, ss, sr, cs, cr,
):
    rows, width = q_hbm.shape
    hd = 128
    full = HEADS * hd
    scale = hd ** (-0.5)
    half = rows // 2
    n_head = HEADS * hd // width
    sets = (0, 1)
    me_seq = lax.axis_index("seq")
    me_head = lax.axis_index("head")
    core = me_seq % 2
    mine = pl.ds(pl.multiple_of(core * hd, hd), hd)
    other = pl.ds(pl.multiple_of((1 - core) * hd, hd), hd)

    seq_peer = {j: {"seq": flipped(me_seq, j)} for j in (7, 6, 5, 4, 3, 2, 1)}
    head_peer = {j: {"head": (me_head + j) % n_head} for j in (2, 1, 3)}
    cross_peer = {j: {**seq_peer[1], **head_peer[j]} for j in head_peer}
    peers = list(cross_peer.values()) + list(head_peer.values()) + list(seq_peer.values())
    barrier = pltpu.get_barrier_semaphore()
    for peer in peers:
        pl.semaphore_signal(barrier, inc=1, device_id=peer, device_id_type=pl.DeviceIdType.MESH)

    loads = []

    def load(src, dst):
        copy = pltpu.make_async_copy(src, dst, in_sem.at[len(loads)])
        copy.start()
        loads.append(copy)
        return copy

    kv_loads = []
    for i, ref in enumerate((k_hbm, v_hbm)):
        kv_loads.append(load(ref.at[:, mine], near.at[i, 0, pl.ds(0, rows)]))
        kv_loads.append(load(ref.at[:, other], given.at[i]))
    q_loads = [load(q_hbm.at[:, mine], qh.at[0]), load(q_hbm.at[:, other], given.at[2])]
    co_loads = [load(co_hbm.at[:, mine], coh.at[0]), load(co_hbm.at[:, other], given.at[3])]
    gain_load = load(gain_hbm, gain_ref)

    sent = []

    def send(src, dst, send_sem, recv_sem, peer):
        copy = pltpu.make_async_remote_copy(
            src_ref=src, dst_ref=dst, send_sem=send_sem, recv_sem=recv_sem,
            device_id=peer, device_id_type=pl.DeviceIdType.MESH,
        )
        copy.start()
        sent.append(copy)
        return copy

    def swap(n, src, dst):
        return send(src, dst, cs.at[n], cr.at[n], seq_peer[1])

    r = lax.broadcasted_iota(jnp.int32, (448, rows), 0)
    c = lax.broadcasted_iota(jnp.int32, (448, rows), 1)
    low = jnp.where(r < 256, 2 * r, jnp.where(r < 384, 4 * (r - 256), 8 * (r - 384)))
    size = jnp.where(r < 256, 2, jnp.where(r < 384, 4, 8))
    weight = jnp.where(r < 256, 0.5, jnp.where(r < 384, 0.25, 0.125))
    averages = jnp.where((c >= low) & (c < low + size), weight, 0.0).astype(jnp.bfloat16)

    linked = {}
    for i in range(2):
        kv_loads[2 * i].wait()
        kv_loads[2 * i + 1].wait()
        both = mm(averages, jnp.concatenate([near[i, 0, 0:rows, :], given[i]], axis=1)).astype(jnp.bfloat16)
        coarse[0, i] = both[:, 0:hd]
        coarse[1, i] = both[:, hd:]
        near[i, 1, rows : rows + 256, :] = both[0:256, 0:hd]
        if i == 0:
            pl.semaphore_wait(barrier, len(peers))
        for j, (at, count, own, _) in LINKED.items():
            linked[i, j] = send(
                coarse.at[j % 2, i, pl.ds(own, count)], far.at[i, pl.ds(at, count)],
                fs.at[i, j - 2], fr.at[i, j - 2], seq_peer[j],
            )
    for copy in q_loads + co_loads:
        copy.wait()
    swapped = [swap(i, given.at[i], near.at[i, 1, pl.ds(0, rows)]) for i in range(2)]
    swapped += [swap(2, given.at[2], qh.at[1]), swap(3, given.at[3], coh.at[1])]

    def transposed_rows(i, t, block):
        at, count = block
        near_t[i, t, :, at : at + count] = near[i, t, at : at + count, :].T

    m_run, l_run, m_used = {}, {}, {}

    def near_block(block, t, qh_at):
        at, count = block
        q_rows = slice(qh_at * half, (qh_at + 1) * half)
        s = mm(near[0, t, at : at + count, :], qh[t, q_rows, :], NT) * (scale * LOG2E)
        top = jnp.max(s, axis=0, keepdims=True)
        if block == TWIN:
            top = jnp.maximum(top, m_run[t, qh_at])
        p = jnp.exp2(s - top)
        total = jnp.sum(p, axis=0, keepdims=True)
        p = p.astype(jnp.bfloat16)
        pt[t, at : at + count, q_rows] = p
        o = mm(near_t[1, t, :, at : at + count], p)
        if block == TWIN:
            alpha = jnp.exp2(m_run[t, qh_at] - top)
            total = total + l_run[t, qh_at] * alpha
            o = o + ot[t, :, q_rows] * alpha
        ot[t, :, q_rows] = o
        m_run[t, qh_at] = top
        l_run[t, qh_at] = total
        m_used[block, t, qh_at] = top

    def near_blocks(block, t):
        transposed_rows(1, t, block)
        for qh_at in range(2):
            near_block(block, t, qh_at)

    near_blocks(LOCAL, 0)
    for copy in swapped:
        copy.wait_recv()
    for i in range(2):
        near[i, 0, rows : rows + 256, :] = mm(averages[0:256], near[i, 1, 0:rows, :]).astype(jnp.bfloat16)
    near_blocks(LOCAL, 1)
    near_blocks(TWIN, 1)
    near_blocks(TWIN, 0)

    gain_load.wait()
    gain = gain_ref[:, mine]
    gain_t = jnp.broadcast_to(gain, (hd, hd)).T
    for t in sets:
        gcot[t] = (coh[t].astype(jnp.float32) * gain).T

    for j in LINKED:
        linked[0, j].wait_recv()
    lse = {}
    for t in sets:
        m_near = jnp.concatenate([m_run[t, 0], m_run[t, 1]], axis=1)
        l_near = jnp.concatenate([l_run[t, 0], l_run[t, 1]], axis=1)
        pf[...] = mm(far[0], qh[t], NT) * (scale * LOG2E)
        top = jnp.maximum(m_near, jnp.max(pf[...], axis=0, keepdims=True))
        p = jnp.exp2(pf[...] - top)
        pf[...] = p
        total = l_near * jnp.exp2(m_near - top) + jnp.sum(p, axis=0, keepdims=True)
        lse[t] = top + jnp.log2(total)
        pt[t, 768:1280, :] = (pf[...] * (1.0 / total)).astype(jnp.bfloat16)
        ot[t] = ot[t] * jnp.exp2(m_near - lse[t])
    far_t[0] = far[0].T
    for t in sets:
        transposed_rows(0, t, LOCAL)
        transposed_rows(0, t, TWIN)

    for j in LINKED:
        linked[1, j].wait_recv()
    far_t[1] = far[1].T
    for t in sets:
        o = (ot[t] + mm(far_t[1], pt[t, 768:1280, :])).astype(jnp.bfloat16).astype(jnp.float32)
        ot[t] = o
        square = jnp.sum(o * o, axis=0, keepdims=True)
        inner = jnp.sum(o * gcot[t], axis=0, keepdims=True)
        for part in range(rows // 128):
            lanes = slice(part * 128, (part + 1) * 128)
            stats[t, part : part + 1, :] = square[:, lanes]
            stats[t, 4 + part : 5 + part, :] = inner[:, lanes]

    def send_stats(slot, peer):
        return send(stats, stats_in.at[slot], ss.at[slot], sr.at[slot], peer)

    stat_copies = [send_stats(j + 2, cross_peer[j]) for j in head_peer] + [send_stats(j - 1, head_peer[j]) for j in head_peer]
    stat_copies.append(send_stats(6, seq_peer[1]))
    for copy in stat_copies:
        copy.wait_recv()
    inverse, slope = {}, {}
    for t in sets:
        both = stats[t] + stats_in[0, t] + stats_in[1, t] + stats_in[2, t]
        both = both + (stats_in[3, 1 - t] + stats_in[4, 1 - t] + stats_in[5, 1 - t] + stats_in[6, 1 - t])
        square = jnp.concatenate([both[i : i + 1] for i in range(4)], axis=1)
        inner = jnp.concatenate([both[i : i + 1] for i in range(4, 8)], axis=1)
        inverse[t] = lax.rsqrt(square * (1.0 / full) + NORM_EPS)
        slope[t] = inverse[t] * inverse[t] * inverse[t] * inner * (1.0 / full)

    FAR_G = 2
    for t in sets:
        gb[FAR_G, t] = (gcot[t] * inverse[t] - ot[t] * slope[t]).astype(jnp.bfloat16)
    back = {}

    def send_back(i):
        for j, (at, count, _, to) in LINKED.items():
            back[i, j] = send(
                cot_out.at[i, pl.ds(at, count)], cot_in.at[j % 2, i, pl.ds(to, count)],
                bs.at[i, j - 2], br.at[i, j - 2], seq_peer[j],
            )

    cot_out[1] = (
        mm(pt[0, 768:1280, :], gb[FAR_G, 0], NT) + mm(pt[1, 768:1280, :], gb[FAR_G, 1], NT)
    ).astype(jnp.bfloat16)
    send_back(1)

    def score_cot(p, values, g, d_row):
        return (p.astype(jnp.float32) * (mm(values, g) - d_row)).astype(jnp.bfloat16)

    delta = {}
    dk = None
    for t in sets:
        g = gb[FAR_G, t]
        delta[t] = jnp.sum(g.astype(jnp.float32) * ot[t], axis=0, keepdims=True)
        ds = score_cot(pt[t, 768:1280, :], far[1], g, delta[t])
        pt[t, 768:1280, :] = ds
        part = mm(ds, qh[t])
        dk = part if dk is None else dk + part
    cot_out[0] = (dk * scale).astype(jnp.bfloat16)
    send_back(0)

    near_delta = {}
    for t in sets:
        dqt[t] = mm(far_t[0], pt[t, 768:1280, :])
        o = ot[t]
        g = gcot[t] * inverse[t] - o * slope[t]
        for n, block in enumerate((LOCAL, TWIN)):
            e = jnp.exp2(jnp.concatenate([m_used[block, t, 0], m_used[block, t, 1]], axis=1) - lse[t])
            gb[n, t] = (g * e).astype(jnp.bfloat16)
            near_delta[block, t] = delta[t] * e

    def near_cots(block, t):
        at, count = block
        g = gb[(LOCAL, TWIN).index(block), t]
        p = pt[t, at : at + count, :]
        ds = score_cot(p, near[1, t, at : at + count, :], g, near_delta[block, t])
        dqt[t] = dqt[t] + mm(near_t[0, t, :, at : at + count], ds)
        return mm(ds, qh[t]) * scale, mm(p, g, NT)

    r = lax.broadcasted_iota(jnp.int32, (rows, 256), 0)
    c = lax.broadcasted_iota(jnp.int32, (rows, 256), 1)
    halves = jnp.where(r // 2 == c, 0.5, 0.0).astype(jnp.bfloat16)
    for t in (0, 1):
        twin_k, twin_v = near_cots(TWIN, t)
        twin_cot[1 - t, :, 0:hd] = twin_k.astype(jnp.bfloat16)
        twin_cot[1 - t, :, hd:] = twin_v.astype(jnp.bfloat16)
    handed = []
    for t in (1, 0):
        local_k, local_v = near_cots(LOCAL, t)
        total = mm(halves, twin_cot[t])
        normed = (ot[t] * inverse[t] * jnp.concatenate([gain_t] * (rows // 128), axis=1)).T.astype(jnp.bfloat16)
        dq = (dqt[t] * scale).T.astype(jnp.bfloat16)
        if t == 1:
            back_out[2, :, :] = (local_k + total[:, 0:hd]).astype(jnp.bfloat16)
            back_out[3, :, :] = (local_v + total[:, hd:]).astype(jnp.bfloat16)
            back_out[0, :, :] = normed
            back_out[1, :, :] = dq
            handed.append(swap(4, back_out, back_in))
        else:
            acc[0] = local_k + total[:, 0:hd]
            acc[1] = local_v + total[:, hd:]
            norm_out[:, mine] = normed
            dq_out[:, mine] = dq
    handed[0].wait_recv()
    norm_out[:, other] = back_in[0]
    dq_out[:, other] = back_in[1]

    low = jnp.where(c < 128, 4 * c, 8 * ((c - 128) % 64))
    size = jnp.where(c < 128, 4, 8)
    weight = jnp.where(c < 128, 0.25, 0.125)
    others = jnp.where((r >= low) & (r < low + size), weight, 0.0).astype(jnp.bfloat16)
    for i, out in ((1, dv_out), (0, dk_out)):
        for j in LINKED:
            back[i, j].wait_recv()
        added = mm(others, jnp.concatenate([cot_in[0, i], cot_in[1, i]], axis=1))
        out[:, mine] = (acc[i] + added[:, 0:hd]).astype(jnp.bfloat16)
        out[:, other] = (back_in[2 + i].astype(jnp.float32) + added[:, hd:]).astype(jnp.bfloat16)

    for copy in sent:
        copy.wait_send()


def store_kernel(*refs):
    copies = [pltpu.make_async_copy(refs[i], refs[4 + i], refs[8].at[i]) for i in range(4)]
    for copy in copies:
        copy.start()
    for copy in copies:
        copy.wait()


def on_device(queries, key_tokens, value_tokens, norm_gain, out_cotangent):
    rows, width = queries.shape
    hd = 128
    bf, f32 = jnp.bfloat16, jnp.float32
    hbm = pl.BlockSpec(memory_space=pltpu.HBM)
    vmem = pl.BlockSpec(memory_space=pltpu.VMEM)
    dma = pltpu.SemaphoreType.DMA
    in_hbm = functools.partial(pltpu.with_memory_space_constraint, memory_space=pltpu.HBM)
    in_vmem = functools.partial(pltpu.with_memory_space_constraint, memory_space=pltpu.VMEM)
    results = pl.pallas_call(
        kernel,
        out_shape=(pltpu.VMEM((rows, width), bf),) * 4,
        in_specs=[hbm] * 5,
        out_specs=(vmem,) * 4,
        scratch_shapes=[
            pltpu.VMEM((2, 2, rows + 256, hd), bf),
            pltpu.VMEM((2, 512, hd), bf),
            pltpu.VMEM((2, 2, hd, rows + 256), bf),
            pltpu.VMEM((2, hd, 512), bf),
            pltpu.VMEM((4, rows, hd), bf),
            pltpu.VMEM((2, rows, hd), bf),
            pltpu.VMEM((2, rows, hd), bf),
            pltpu.VMEM((1, width), f32),
            pltpu.VMEM((2, 2, 448, hd), bf),
            pltpu.VMEM((2, 512, hd), bf),
            pltpu.VMEM((2, 2, 256, hd), bf),
            pltpu.VMEM((2, rows + 768, rows), bf),
            pltpu.VMEM((512, rows), f32),
            pltpu.VMEM((2, hd, rows), f32),
            pltpu.VMEM((2, hd, rows), f32),
            pltpu.VMEM((3, 2, hd, rows), bf),
            pltpu.VMEM((2, hd, rows), f32),
            pltpu.VMEM((2, 8, 128), f32),
            pltpu.VMEM((7, 2, 8, 128), f32),
            pltpu.VMEM((2, rows, hd), f32),
            pltpu.VMEM((4, rows, hd), bf),
            pltpu.VMEM((4, rows, hd), bf),
            pltpu.VMEM((2, 256, 2 * hd), bf),
            dma((9,)), dma((2, 6)), dma((2, 6)), dma((2, 6)), dma((2, 6)), dma((7,)), dma((7,)), dma((5,)), dma((5,)),
        ],
        compiler_params=pltpu.CompilerParams(
            collective_id=0, has_side_effects=True, vmem_limit_bytes=48 * 2**20
        ),
    )(in_hbm(queries), in_hbm(key_tokens), in_hbm(value_tokens), in_hbm(norm_gain.reshape(1, width)), in_hbm(out_cotangent))
    return pl.pallas_call(
        store_kernel,
        out_shape=(pltpu.HBM((rows, width), bf),) * 4,
        in_specs=[vmem] * 4,
        out_specs=(hbm,) * 4,
        scratch_shapes=[dma((4,))],
    )(*[in_vmem(result) for result in results])


def solution(mesh):
    return jax.shard_map(
        on_device,
        mesh=mesh,
        in_specs=(P("seq", "head"), P("seq", "head"), P("seq", "head"), P("head"), P("seq", "head")),
        out_specs=(P("seq", "head"),) * 4,
        check_vma=False,
    )
```

time: 32.2 us -> 30.8 us (0.957)
  Pallas kernels: 31.5 us -> 30 us
    pallas_call x1, Pallas kernels: 30.5 us -> 29 us  [on_device(): pl.pallas_call(kernel, out_shape=(pltpu.VMEM((rows, width), bf),) * 4, in...]
where the time goes in v3:
time: 30.8 us; the launch traced here: 30.7 us
  Pallas kernels  30 us (97%)
  between operations  0.64 us (2%)
    pallas_call x1, Pallas kernels, on_device(): pl.pallas_call(kernel, out_shape=(pltpu.VMEM((rows, width), bf),) * 4, in...  29 us
    pallas_call x1, Pallas kernels, on_device(): pl.pallas_call(store_kernel, out_shape=(pltpu.HBM((rows, width), bf),) *...  1 us

profile of v3, /device:TPU:1, one launch (start us, length us, event | category | flops | bytes accessed | tf_op | source)
XLA Modules:
  0.0 30.7 jit_solution(1175788620876472005)
XLA Ops:
  0.6 29.0 %shard_map.84 = (bf16[512,256]{1,0:T(8,128)(2,1)S(1)}, bf16[512,256]{1,0:T(8,128)(2,1)S(1)}, bf16[512,256]{1,0:T(8,128)(2,1)S(1)}, bf16[512,256]{1,0:T(8,128)(2,1)S(1)}) custom-call(bf16[512,256]{1,0:T(8,128)(2,1)} %q_hbm.1, bf16[512,256]{1,0:T(8,128)(2,1)} %k_hbm.1, bf16[512,256]{1,0:T(8,128)(2,1)} %v_hbm.1, f32[1,256]{1,0:T(1,128)} %bitcast.1, ...), custom_call_target="tpu_custom_call" | custom-call | tf_op jit(solution)/shard_map/pallas_call | solution.py:325
  29.7 1.0 %shard_map.85 = (bf16[512,256]{1,0:T(8,128)(2,1)}, bf16[512,256]{1,0:T(8,128)(2,1)}, bf16[512,256]{1,0:T(8,128)(2,1)}, bf16[512,256]{1,0:T(8,128)(2,1)}) custom-call(bf16[512,256]{1,0:T(8,128)(2,1)S(1)} %get-tuple-element.8.refs_0_, bf16[512,256]{1,0:T(8,128)(2,1)S(1)} %get-tuple-element.9.refs_1_, bf16[512,256]{1,0:T(8,128)(2,1)S(1)} %get-tuple-element.10.refs_2_, ...), custom_call_target="tpu_custom_call" | custom-call | tf_op jit(solution)/shard_map/pallas_call | solution.py:360

commit v4 on v3

--- a/solution.py
+++ b/solution.py
@@ -37,7 +37,7 @@
     norm_out, dq_out, dk_out, dv_out,
     near, far, near_t, far_t, given, qh, coh, gain_ref, coarse, cot_out, cot_in, pt, pf, gcot, ot, gb, dqt, stats, stats_in,
     acc, back_out, back_in, twin_cot,
-    in_sem, fs, fr, bs, br, ss, sr, cs, cr,
+    in_sem, fs, fr, bs, br, ss, sr, cs, cr, ready,
 ):
     rows, width = q_hbm.shape
     hd = 128
@@ -55,10 +55,36 @@
     seq_peer = {j: {"seq": flipped(me_seq, j)} for j in (7, 6, 5, 4, 3, 2, 1)}
     head_peer = {j: {"head": (me_head + j) % n_head} for j in (2, 1, 3)}
     cross_peer = {j: {**seq_peer[1], **head_peer[j]} for j in head_peer}
-    peers = list(cross_peer.values()) + list(head_peer.values()) + list(seq_peer.values())
+
+    place = me_seq % 8
+    is_lead = place == 0
+    is_hub = (me_head == 0) & (core == 0)
     barrier = pltpu.get_barrier_semaphore()
-    for peer in peers:
-        pl.semaphore_signal(barrier, inc=1, device_id=peer, device_id_type=pl.DeviceIdType.MESH)
+
+    def signal(semaphore, peer):
+        pl.semaphore_signal(semaphore, inc=1, device_id=peer, device_id_type=pl.DeviceIdType.MESH)
+
+    @pl.when(jnp.logical_not(is_lead))
+    def _():
+        for peer in seq_peer.values():
+            signal(barrier, peer)
+
+    @pl.when(me_head != 0)
+    def _():
+        signal(barrier, {"seq": me_seq - core, "head": 0})
+
+    def enter():
+        pl.semaphore_wait(barrier, 6 + jnp.where(is_lead, 1, 0) + jnp.where(is_hub, 6, 0))
+
+        @pl.when(is_lead)
+        def _():
+            for peer in seq_peer.values():
+                signal(ready.at[0], peer)
+
+        @pl.when(is_hub)
+        def _():
+            for peer in list(cross_peer.values()) + list(head_peer.values()) + [seq_peer[1]]:
+                signal(ready.at[1], peer)
 
     loads = []
 
@@ -78,13 +104,17 @@
 
     sent = []
 
-    def send(src, dst, send_sem, recv_sem, peer):
+    def prepare(src, dst, send_sem, recv_sem, peer):
         copy = pltpu.make_async_remote_copy(
             src_ref=src, dst_ref=dst, send_sem=send_sem, recv_sem=recv_sem,
             device_id=peer, device_id_type=pl.DeviceIdType.MESH,
         )
+        sent.append(copy)
+        return copy
+
+    def send(*copy_args):
+        copy = prepare(*copy_args)
         copy.start()
-        sent.append(copy)
         return copy
 
     def swap(n, src, dst):
@@ -106,16 +136,33 @@
         coarse[1, i] = both[:, hd:]
         near[i, 1, rows : rows + 256, :] = both[0:256, 0:hd]
         if i == 0:
-            pl.semaphore_wait(barrier, len(peers))
+            enter()
         for j, (at, count, own, _) in LINKED.items():
-            linked[i, j] = send(
+            linked[i, j] = prepare(
                 coarse.at[j % 2, i, pl.ds(own, count)], far.at[i, pl.ds(at, count)],
                 fs.at[i, j - 2], fr.at[i, j - 2], seq_peer[j],
             )
+            pl.when(place != j)(linked[i, j].start)
     for copy in q_loads + co_loads:
         copy.wait()
-    swapped = [swap(i, given.at[i], near.at[i, 1, pl.ds(0, rows)]) for i in range(2)]
-    swapped += [swap(2, given.at[2], qh.at[1]), swap(3, given.at[3], coh.at[1])]
+    swapped = []
+    for n, dst in enumerate((near.at[0, 1, pl.ds(0, rows)], near.at[1, 1, pl.ds(0, rows)], qh.at[1], coh.at[1])):
+        swapped.append(prepare(given.at[n], dst, cs.at[n], cr.at[n], seq_peer[1]))
+
+    def start_swaps():
+        for copy in swapped:
+            copy.start()
+
+    pl.when(place != 1)(start_swaps)
+
+    @pl.when(jnp.logical_not(is_lead))
+    def _():
+        pl.semaphore_wait(ready.at[0], 1)
+
+    for i in range(2):
+        for j in LINKED:
+            pl.when(place == j)(linked[i, j].start)
+    pl.when(place == 1)(start_swaps)
 
     def transposed_rows(i, t, block):
         at, count = block
@@ -195,6 +242,10 @@
             lanes = slice(part * 128, (part + 1) * 128)
             stats[t, part : part + 1, :] = square[:, lanes]
             stats[t, 4 + part : 5 + part, :] = inner[:, lanes]
+
+    @pl.when(jnp.logical_not(is_hub))
+    def _():
+        pl.semaphore_wait(ready.at[1], 1)
 
     def send_stats(slot, peer):
         return send(stats, stats_in.at[slot], ss.at[slot], sr.at[slot], peer)
@@ -352,6 +403,7 @@
             pltpu.VMEM((4, rows, hd), bf),
             pltpu.VMEM((2, 256, 2 * hd), bf),
             dma((9,)), dma((2, 6)), dma((2, 6)), dma((2, 6)), dma((2, 6)), dma((7,)), dma((7,)), dma((5,)), dma((5,)),
+            pltpu.SemaphoreType.REGULAR((2,)),
         ],
         compiler_params=pltpu.CompilerParams(
             collective_id=0, has_side_effects=True, vmem_limit_bytes=48 * 2**20

time: 30.8 us -> 28.5 us (0.925)
  Pallas kernels: 30 us -> 27.7 us
    pallas_call x1, Pallas kernels: 29 us -> 26.7 us  [on_device(): pl.pallas_call(kernel, out_shape=(pltpu.VMEM((rows, width), bf),) * 4, in...]
where the time goes in v4:
time: 28.5 us; the launch traced here: 28.4 us
  Pallas kernels  27.7 us (97%)
  between operations  0.64 us (2%)
    pallas_call x1, Pallas kernels, on_device(): pl.pallas_call(kernel, out_shape=(pltpu.VMEM((rows, width), bf),) * 4, in...  26.7 us
    pallas_call x1, Pallas kernels, on_device(): pl.pallas_call(store_kernel, out_shape=(pltpu.HBM((rows, width), bf),) *...  1 us

profile of v4, /device:TPU:1, one launch (start us, length us, event | category | flops | bytes accessed | tf_op | source)
XLA Modules:
  0.0 28.4 jit_solution(17741396877400630545)
XLA Ops:
  0.6 26.7 %shard_map.84 = (bf16[512,256]{1,0:T(8,128)(2,1)S(1)}, bf16[512,256]{1,0:T(8,128)(2,1)S(1)}, bf16[512,256]{1,0:T(8,128)(2,1)S(1)}, bf16[512,256]{1,0:T(8,128)(2,1)S(1)}) custom-call(bf16[512,256]{1,0:T(8,128)(2,1)} %q_hbm.1, bf16[512,256]{1,0:T(8,128)(2,1)} %k_hbm.1, bf16[512,256]{1,0:T(8,128)(2,1)} %v_hbm.1, f32[1,256]{1,0:T(1,128)} %bitcast.1, ...), custom_call_target="tpu_custom_call" | custom-call | tf_op jit(solution)/shard_map/pallas_call | solution.py:376
  27.4 1.0 %shard_map.85 = (bf16[512,256]{1,0:T(8,128)(2,1)}, bf16[512,256]{1,0:T(8,128)(2,1)}, bf16[512,256]{1,0:T(8,128)(2,1)}, bf16[512,256]{1,0:T(8,128)(2,1)}) custom-call(bf16[512,256]{1,0:T(8,128)(2,1)S(1)} %get-tuple-element.8.refs_0_, bf16[512,256]{1,0:T(8,128)(2,1)S(1)} %get-tuple-element.9.refs_1_, bf16[512,256]{1,0:T(8,128)(2,1)S(1)} %get-tuple-element.10.refs_2_, ...), custom_call_target="tpu_custom_call" | custom-call | tf_op jit(solution)/shard_map/pallas_call | solution.py:412

commit v5 on v4

--- a/solution.py
+++ b/solution.py
@@ -58,7 +58,8 @@
 
     place = me_seq % 8
     is_lead = place == 0
-    is_hub = (me_head == 0) & (core == 0)
+    hub_head = jnp.where(me_seq < 2, 0, 2)
+    is_hub = (me_head == hub_head) & (core == 0)
     barrier = pltpu.get_barrier_semaphore()
 
     def signal(semaphore, peer):
@@ -69,17 +70,12 @@
         for peer in seq_peer.values():
             signal(barrier, peer)
 
-    @pl.when(me_head != 0)
+    @pl.when(me_head != hub_head)
     def _():
-        signal(barrier, {"seq": me_seq - core, "head": 0})
+        signal(barrier, {"seq": me_seq - core, "head": hub_head})
 
     def enter():
         pl.semaphore_wait(barrier, 6 + jnp.where(is_lead, 1, 0) + jnp.where(is_hub, 6, 0))
-
-        @pl.when(is_lead)
-        def _():
-            for peer in seq_peer.values():
-                signal(ready.at[0], peer)
 
         @pl.when(is_hub)
         def _():
@@ -119,6 +115,12 @@
 
     def swap(n, src, dst):
         return send(src, dst, cs.at[n], cr.at[n], seq_peer[1])
+
+    @pl.when(is_lead)
+    def _():
+        enter()
+        for peer in seq_peer.values():
+            signal(ready.at[0], peer)
 
     r = lax.broadcasted_iota(jnp.int32, (448, rows), 0)
     c = lax.broadcasted_iota(jnp.int32, (448, rows), 1)
@@ -136,7 +138,7 @@
         coarse[1, i] = both[:, hd:]
         near[i, 1, rows : rows + 256, :] = both[0:256, 0:hd]
         if i == 0:
-            enter()
+            pl.when(jnp.logical_not(is_lead))(enter)
         for j, (at, count, own, _) in LINKED.items():
             linked[i, j] = prepare(
                 coarse.at[j % 2, i, pl.ds(own, count)], far.at[i, pl.ds(at, count)],
@@ -146,7 +148,7 @@
     for copy in q_loads + co_loads:
         copy.wait()
     swapped = []
-    for n, dst in enumerate((near.at[0, 1, pl.ds(0, rows)], near.at[1, 1, pl.ds(0, rows)], qh.at[1], coh.at[1])):
+    for n, dst in ((0, near.at[0, 1, pl.ds(0, rows)]), (2, qh.at[1]), (1, near.at[1, 1, pl.ds(0, rows)]), (3, coh.at[1])):
         swapped.append(prepare(given.at[n], dst, cs.at[n], cr.at[n], seq_peer[1]))
 
     def start_swaps():
@@ -197,7 +199,7 @@
             near_block(block, t, qh_at)
 
     near_blocks(LOCAL, 0)
-    for copy in swapped:
+    for copy in swapped[:3]:
         copy.wait_recv()
     for i in range(2):
         near[i, 0, rows : rows + 256, :] = mm(averages[0:256], near[i, 1, 0:rows, :]).astype(jnp.bfloat16)
@@ -206,6 +208,7 @@
     near_blocks(TWIN, 0)
 
     gain_load.wait()
+    swapped[3].wait_recv()
     gain = gain_ref[:, mine]
     gain_t = jnp.broadcast_to(gain, (hd, hd)).T
     for t in sets:
@@ -230,11 +233,16 @@
         transposed_rows(0, t, LOCAL)
         transposed_rows(0, t, TWIN)
 
-    for j in LINKED:
+    for j in (7, 6, 5, 4):
         linked[1, j].wait_recv()
-    far_t[1] = far[1].T
-    for t in sets:
-        o = (ot[t] + mm(far_t[1], pt[t, 768:1280, :])).astype(jnp.bfloat16).astype(jnp.float32)
+    far_t[1, :, 256:512] = far[1, 256:512, :].T
+    for t in sets:
+        ot[t] = ot[t] + mm(far_t[1, :, 256:512], pt[t, 1024:1280, :])
+    for j in (3, 2):
+        linked[1, j].wait_recv()
+    far_t[1, :, 0:256] = far[1, 0:256, :].T
+    for t in sets:
+        o = (ot[t] + mm(far_t[1, :, 0:256], pt[t, 768:1024, :])).astype(jnp.bfloat16).astype(jnp.float32)
         ot[t] = o
         square = jnp.sum(o * o, axis=0, keepdims=True)
         inner = jnp.sum(o * gcot[t], axis=0, keepdims=True)
@@ -250,7 +258,9 @@
     def send_stats(slot, peer):
         return send(stats, stats_in.at[slot], ss.at[slot], sr.at[slot], peer)
 
-    stat_copies = [send_stats(j + 2, cross_peer[j]) for j in head_peer] + [send_stats(j - 1, head_peer[j]) for j in head_peer]
+    stat_copies = []
+    for j in head_peer:
+        stat_copies += [send_stats(j + 2, cross_peer[j]), send_stats(j - 1, head_peer[j])]
     stat_copies.append(send_stats(6, seq_peer[1]))
     for copy in stat_copies:
         copy.wait_recv()
@@ -268,17 +278,19 @@
         gb[FAR_G, t] = (gcot[t] * inverse[t] - ot[t] * slope[t]).astype(jnp.bfloat16)
     back = {}
 
-    def send_back(i):
-        for j, (at, count, _, to) in LINKED.items():
+    def send_back(i, partners):
+        for j in partners:
+            at, count, _, to = LINKED[j]
             back[i, j] = send(
                 cot_out.at[i, pl.ds(at, count)], cot_in.at[j % 2, i, pl.ds(to, count)],
                 bs.at[i, j - 2], br.at[i, j - 2], seq_peer[j],
             )
 
-    cot_out[1] = (
-        mm(pt[0, 768:1280, :], gb[FAR_G, 0], NT) + mm(pt[1, 768:1280, :], gb[FAR_G, 1], NT)
-    ).astype(jnp.bfloat16)
-    send_back(1)
+    for at, partners in ((256, (7, 6, 5, 4)), (0, (3, 2))):
+        p_rows = slice(768 + at, 1024 + at)
+        dv = mm(pt[0, p_rows, :], gb[FAR_G, 0], NT) + mm(pt[1, p_rows, :], gb[FAR_G, 1], NT)
+        cot_out[1, at : at + 256, :] = dv.astype(jnp.bfloat16)
+        send_back(1, partners)
 
     def score_cot(p, values, g, d_row):
         return (p.astype(jnp.float32) * (mm(values, g) - d_row)).astype(jnp.bfloat16)
@@ -293,7 +305,7 @@
         part = mm(ds, qh[t])
         dk = part if dk is None else dk + part
     cot_out[0] = (dk * scale).astype(jnp.bfloat16)
-    send_back(0)
+    send_back(0, LINKED)
 
     near_delta = {}
     for t in sets:

time: 28.5 us -> 28.4 us (level)
  no operation moved by 1% of the time
where the time goes in v5:
time: 28.4 us; the launch traced here: 28.3 us
  Pallas kernels  27.6 us (97%)
  between operations  0.64 us (2%)
    pallas_call x1, Pallas kernels, on_device(): pl.pallas_call(kernel, out_shape=(pltpu.VMEM((rows, width), bf),) * 4, in...  26.6 us
    pallas_call x1, Pallas kernels, on_device(): pl.pallas_call(store_kernel, out_shape=(pltpu.HBM((rows, width), bf),) *...  1 us

profile of v5, /device:TPU:1, one launch (start us, length us, event | category | flops | bytes accessed | tf_op | source)
XLA Modules:
  0.0 28.3 jit_solution(7002243120325592466)
XLA Ops:
  0.6 26.6 %shard_map.84 = (bf16[512,256]{1,0:T(8,128)(2,1)S(1)}, bf16[512,256]{1,0:T(8,128)(2,1)S(1)}, bf16[512,256]{1,0:T(8,128)(2,1)S(1)}, bf16[512,256]{1,0:T(8,128)(2,1)S(1)}) custom-call(bf16[512,256]{1,0:T(8,128)(2,1)} %q_hbm.1, bf16[512,256]{1,0:T(8,128)(2,1)} %k_hbm.1, bf16[512,256]{1,0:T(8,128)(2,1)} %v_hbm.1, f32[1,256]{1,0:T(1,128)} %bitcast.1, ...), custom_call_target="tpu_custom_call" | custom-call | tf_op jit(solution)/shard_map/pallas_call | solution.py:388
  27.3 1.0 %shard_map.85 = (bf16[512,256]{1,0:T(8,128)(2,1)}, bf16[512,256]{1,0:T(8,128)(2,1)}, bf16[512,256]{1,0:T(8,128)(2,1)}, bf16[512,256]{1,0:T(8,128)(2,1)}) custom-call(bf16[512,256]{1,0:T(8,128)(2,1)S(1)} %get-tuple-element.8.refs_0_, bf16[512,256]{1,0:T(8,128)(2,1)S(1)} %get-tuple-element.9.refs_1_, bf16[512,256]{1,0:T(8,128)(2,1)S(1)} %get-tuple-element.10.refs_2_, ...), custom_call_target="tpu_custom_call" | custom-call | tf_op jit(solution)/shard_map/pallas_call | solution.py:424
